TPU v7x, 32 devices: a whole 2x2x4 slice. The times are simulated.
32 devices in a mesh: groups: 2 (over y), field: 4 (over x, core), wave: 4 (over z).
Axes of the slice: x: 2, y: 2, z: 4, core: 2. Of those that a mesh axis runs over, the one named last changes fastest.
Arguments:
- mode_basis: bfloat16 [22, 512, 512], P(None, 'wave'), may hold values from -6 to 6
- coef_table: bfloat16 [4096, 22], replicated, may hold values from -1.5 to 1.5
- table_index: int32 [64], P(('groups', 'field')), parts along dimension 0, may hold values from 0 to 4095
- wave_lengths: float32 [8], P('wave'), may hold values from 0.32 to 1.05
- sed_table: float32 [1024, 8], replicated, may hold values from 0.05 to 1
- template_ids: int32 [64, 8], P(('groups', 'field')), parts along dimension 0, may hold values from 0 to 1023
Outputs:
- mixed: bfloat16 [64, 8, 256, 256], P(('groups', 'field'), None, 'wave'), parts along dimension 0
There are 2 independent parts, one for each index of `groups`. A program takes and returns all parts, laid end to end along the dimension named above; an argument that names none is the same for every part. Nothing has to cross between parts.
All inputs are finite; a program needn't handle non-finite values.
Results may differ from a plain program's by a relative error of at most 0.0065.
Values may be sent and summed in bfloat16 or wider, within the bound.
A program may use at most 128 MiB of HBM per device.

v0:
```python
import functools

import jax
import jax.numpy as jnp
import numpy as np
from jax import lax
from jax.experimental import pallas as pl
from jax.experimental.pallas import tpu as pltpu
from jax.sharding import PartitionSpec as P

PUP = 512
PIX = 256
EPSILON = 1e-06
GROUP = 16
ROUNDER = 12582912.0


def turns_sincos(turns):
    nearest = (turns + ROUNDER) - ROUNDER
    r = turns - nearest
    s = r * r
    a = r * SINE(s)
    b = COSINE(s)
    return 1.0 - a * a, a * b


def SINE(s):
    return SIN[0] + s * (SIN[1] + s * (SIN[2] + s * SIN[3]))


def COSINE(s):
    return COS[0] + s * (COS[1] + s * (COS[2] + s * (COS[3] + s * COS[4])))


SIN = (4.442879676818848, -7.307816505432129, 3.5977742671966553, -0.7911993861198425)
COS = (1.4142135381698608, -6.978850841522217, 5.739460468292236, -1.883557915687561, 0.3106880187988281)


def open_patterns(slabs, rows):
    pos = 2 * np.arange(PUP) - PUP + 1
    radius = pos[:, None] ** 2 + pos[None, :] ** 2
    inside = (radius <= PUP * PUP) & (radius >= (61 * PUP // 100) ** 2)
    width = 128
    patterns = {}
    for slab in range(slabs):
        groups = []
        for r in range(slab * rows, (slab + 1) * rows, GROUP):
            spans = []
            for low in range(0, PUP, width):
                if inside[r : r + GROUP, low : low + width].any():
                    if spans and spans[-1][1] == low:
                        spans[-1] = (spans[-1][0], low + width)
                    else:
                        spans.append((low, low + width))
            groups.append(tuple(spans))
        patterns.setdefault(tuple(groups), []).append(slab)
    return patterns


def hop(order, slabs):
    odd = order % 2
    return odd * ((order + 1) // 2) + (1 - odd) * (slabs - order // 2)


def psf_kernel(
    sizes, waves, fields, mix_ref, weight_ref, length_ref, basis_ref, out_ref,
    whole, inverse, path, image, table, efield0, efield1, opening, power, total, arrived,
    local_sem, wl_send, wl_recv, send1, recv1, send2, recv2, send3, recv3, sum_send, sum_recv,
):
    slabs, field_parts, group_parts = sizes
    count, rows, _ = basis_ref.shape
    modes = whole.shape[1]
    upix = PIX // slabs
    own_waves = waves // slabs
    x_parts = field_parts // 2
    chips = x_parts * group_parts
    own = modes // (2 * chips)
    templates = out_ref.shape[1]

    me = lax.axis_index("wave")
    part = lax.axis_index("field")
    core = part % 2
    chip = lax.axis_index("groups") * x_parts + part // 2
    first_pix = me * upix

    def wave_peer(shift):
        return {"wave": (me + shift) % slabs}

    def chip_peer(shift):
        other = (chip + shift) % chips
        return {"groups": other // x_parts, "field": (other % x_parts) * 2 + core}

    sibling = {"field": part + 1 - 2 * core}

    def remote(src, dst, send, recv, device):
        return pltpu.make_async_remote_copy(
            src_ref=src, dst_ref=dst, send_sem=send, recv_sem=recv,
            device_id=device, device_id_type=pl.DeviceIdType.MESH,
        )

    def from_slab(order):
        return (me + 2 * slabs - hop(order, slabs)) % slabs

    def piece(slab, of_chip):
        return whole.at[slab, pl.ds((core * chips + of_chip) * own, own)]

    def first_copy(order):
        shift = hop(order, slabs)
        mine = piece(me, chip)
        return remote(mine, mine, send1.at[order - 1], recv1.at[order - 1], wave_peer(shift))

    def first_landed(order):
        ref = piece(from_slab(order), chip)
        return remote(ref, ref, send1.at[order - 1], recv1.at[order - 1], wave_peer(hop(order, slabs)))

    relay = x_parts == 2 and group_parts == 2
    chip_x, chip_y = chip % x_parts, chip // x_parts
    flip_x, flip_y = 1 - 2 * chip_x, 1 - 2 * chip_y
    first_chip = (chip_y + core * flip_y) * x_parts + chip_x + (1 - core) * flip_x
    second_chip = (chip_y + (1 - core) * flip_y) * x_parts + chip_x + core * flip_x

    def chip_device(other):
        return {"groups": other // x_parts, "field": (other % x_parts) * 2 + core}

    def plane_copy(order, shift):
        at = (order - 1, shift - 1)
        slab = from_slab(order)
        if relay:
            ref = piece(slab, first_chip if shift == 3 else chip)
            device = chip_device(first_chip if shift == 1 else second_chip)
        else:
            ref = piece(slab, chip)
            device = chip_peer(shift)
        return remote(ref, ref, send2.at[at], recv2.at[at], device)

    def plane_landed(order, shift):
        at = (order - 1, shift - 1)
        slab = from_slab(order)
        if relay:
            ref = piece(slab, (first_chip, second_chip, chips - 1 - chip)[shift - 1])
        else:
            ref = piece(slab, (chip + chips - shift) % chips)
        return remote(ref, ref, send2.at[at], recv2.at[at], chip_peer(shift))

    def core_copy(order, which):
        ref = whole.at[from_slab(order), pl.ds(which * chips * own, chips * own)]
        return remote(ref, ref, send3.at[order - 1], recv3.at[order - 1], sibling)

    def length_copy(shift, sender):
        ref = inverse.at[pl.ds(sender * own_waves, own_waves)]
        return remote(ref, ref, wl_send.at[shift - 1], wl_recv.at[shift - 1], wave_peer(shift))

    barrier = pltpu.get_barrier_semaphore()
    peers = [wave_peer(d) for d in range(1, slabs)] + [chip_peer(e) for e in range(1, chips)] + [sibling]
    for peer in peers:
        pl.semaphore_signal(barrier, inc=1, device_id=peer, device_id_type=pl.DeviceIdType.MESH)
    bring = pltpu.make_async_copy(basis_ref, whole.at[me, pl.ds(0, count)], local_sem)
    bring.start()
    if modes > count:
        whole[me, count:, :, :] = jnp.zeros((modes - count, rows, PUP), jnp.bfloat16)
    inverse[pl.ds(me * own_waves, own_waves)] = 1.0 / length_ref[...]
    pl.semaphore_wait(barrier, len(peers))
    for d in range(1, slabs):
        length_copy(d, me).start()
    bring.wait()
    first_copy(1).start()

    def clear(f, carry):
        for l in range(waves):
            image[l, pl.ds(f * upix, upix), :] = jnp.zeros((upix, 2 * PUP), jnp.float32)
        return carry

    lax.fori_loop(0, fields, clear, 0)
    for d in range(1, slabs):
        length_copy(d, (me + slabs - d) % slabs).wait_recv()

    def step_body(step, carry):
        order = step // waves
        wave = step % waves
        slab = from_slab(order)
        first_row = slab * rows

        for o in range(1, slabs):

            @pl.when(step == (o * 3 * waves) // 8 - 1)
            def _():
                first_landed(o).wait_recv()
                if o + 1 < slabs:
                    first_copy(o).wait_send()
                    first_copy(o + 1).start()
                for e in range(1, 3 if relay else chips):
                    plane_copy(o, e).start()

            if relay:

                @pl.when(step == (o * 3 * waves) // 8 + 2)
                def _():
                    plane_landed(o, 1).wait_recv()
                    plane_copy(o, 3).start()

            @pl.when(step == (o * waves - waves // 2 + 1 if o > 1 else waves))
            def _():
                for e in range(2 if relay else 1, chips):
                    plane_landed(o, e).wait_recv()
                core_copy(o, core).start()

            @pl.when(step == o * waves)
            def _():
                core_copy(o, 1 - core).wait_recv()

        @pl.when(wave == 0)
        def _():
            def paths(g, c):
                r = pl.multiple_of(g * GROUP, GROUP)
                block = whole[slab, :, pl.ds(r, GROUP), :].reshape(modes * GROUP, PUP)
                diff = jnp.dot(mix_ref[...], block, preferred_element_type=jnp.float32)
                path[:, pl.ds(r, GROUP), :] = diff.reshape(fields, GROUP, PUP)
                x = 2 * (first_row + r + lax.broadcasted_iota(jnp.int32, (GROUP, PUP), 0)) - PUP + 1
                y = 2 * lax.broadcasted_iota(jnp.int32, (GROUP, PUP), 1) - PUP + 1
                radius = x * x + y * y
                inner = 61 * PUP // 100
                inside = (radius <= PUP * PUP) & (radius >= inner * inner)
                opening[pl.ds(r, GROUP), :] = inside.astype(jnp.float32).astype(jnp.bfloat16)
                return c

            lax.fori_loop(0, rows // GROUP, paths, 0)
            for field in (efield0, efield1):
                field[...] = jnp.zeros_like(field)

        inv = inverse[wave]
        lane = lax.broadcasted_iota(jnp.int32, (upix, 2 * rows), 1)
        real = lane < rows
        xs = 2 * (first_row + jnp.where(real, lane, lane - rows)) - PUP + 1
        us = first_pix + lax.broadcasted_iota(jnp.int32, (upix, 2 * rows), 0) - PIX // 2
        scale = inv[:1, : 2 * rows] * (0.25 / (2.0 * PUP))
        cosine, sine = turns_sincos((us * xs).astype(jnp.float32) * scale)
        kernel = jnp.concatenate(
            [jnp.where(real, cosine, sine), jnp.where(real, -sine, cosine)], axis=0
        ).astype(jnp.bfloat16)
        tile = jnp.concatenate([inv, inv], axis=0)

        def accumulate(f):
            field = (efield0, efield1)[f % 2]
            part_sum = jnp.dot(kernel, field[...], preferred_element_type=jnp.float32)
            here = pl.ds(f * upix, upix)
            image[wave, here, :PUP] += part_sum[:upix]
            image[wave, here, PUP:] += part_sum[upix:]

        def units(pattern):
            for f in range(fields):
                field = (efield0, efield1)[f % 2]
                for group, spans in enumerate(pattern):
                    r = group * GROUP
                    for low, high in spans:
                        turns = path[f, r : r + GROUP, low:high] * tile[:, low:high]
                        cosine, sine = turns_sincos(turns)
                        hole = opening[r : r + GROUP, low:high]
                        field[r : r + GROUP, low:high] = cosine.astype(jnp.bfloat16) * hole
                        field[rows + r : rows + r + GROUP, low:high] = sine.astype(jnp.bfloat16) * hole
                if f > 0:
                    accumulate(f - 1)
            accumulate(fields - 1)

        for pattern, members in open_patterns(slabs, rows).items():
            chosen = slab == members[0]
            for member in members[1:]:
                chosen = chosen | (slab == member)
            pl.when(chosen)(functools.partial(units, pattern))

        return carry

    lax.fori_loop(0, slabs * waves, step_body, 0)

    def finish(wave, carry):
        scale = inverse[wave][:1, :PIX] * (0.25 / (2.0 * PUP))
        step = 64
        for r in range(0, PUP, step):
            ys = 2 * (r + lax.broadcasted_iota(jnp.int32, (step, PIX), 0)) - PUP + 1
            vs = lax.broadcasted_iota(jnp.int32, (step, PIX), 1) - PIX // 2
            cosine, sine = turns_sincos((ys * vs).astype(jnp.float32) * scale)
            cosine = cosine.astype(jnp.bfloat16)
            table[r : r + step, :PIX] = cosine
            table[r : r + step, PIX:] = (-sine).astype(jnp.bfloat16)
            table[PUP + r : PUP + r + step, :PIX] = sine.astype(jnp.bfloat16)
            table[PUP + r : PUP + r + step, PIX:] = cosine
        half = fields * upix // 2
        for h in range(2):
            field = jnp.dot(
                image[wave, h * half : (h + 1) * half, :].astype(jnp.bfloat16),
                table[...],
                preferred_element_type=jnp.float32,
            )
            re, im = field[:, :PIX], field[:, PIX:]
            bright = re * re + im * im
            power[wave, h * half : (h + 1) * half, :] = bright
            sums = jnp.sum(jnp.sum(bright.reshape(fields // 2, upix, PIX), axis=1), axis=1, keepdims=True)
            total[wave, h * (fields // 2) : (h + 1) * (fields // 2), :] = jnp.broadcast_to(
                sums, (fields // 2, PIX)
            )
        return carry

    lax.fori_loop(0, waves, finish, 0)

    def sum_copy(shift):
        return remote(
            total, arrived.at[shift - 1], sum_send.at[shift - 1], sum_recv.at[shift - 1], wave_peer(shift)
        )

    for d in range(1, slabs):
        sum_copy(d).start()
    for d in range(1, slabs):
        sum_copy(d).wait()
    everything = total[...]
    for d in range(1, slabs):
        everything = everything + arrived[d - 1]
    total[...] = 1.0 / (everything * (1.0 / (PIX * PIX)) + EPSILON)

    step = 16

    def mix_fields(f, carry):
        for r in range(0, upix, step):
            sums = [None] * templates
            for l in range(waves):
                level = total[l, pl.ds(f, 1), :]
                bright = power[l, pl.ds(pl.multiple_of(f * upix, step) + r, step), :]
                spectrum = (bright * level).astype(jnp.bfloat16).astype(jnp.float32)
                for j in range(templates):
                    term = spectrum * weight_ref[(f * templates + j) * waves + l]
                    sums[j] = term if l == 0 else sums[j] + term
            for j in range(templates):
                out_ref[f, j, r : r + step, :] = sums[j].astype(jnp.bfloat16)
        return carry

    lax.fori_loop(0, fields, mix_fields, 0)

    for d in range(1, slabs):
        length_copy(d, me).wait_send()
    first_copy(slabs - 1).wait_send()
    for o in range(1, slabs):
        for e in range(1, chips):
            plane_copy(o, e).wait_send()
        core_copy(o, core).wait_send()


def local(sizes, waves, mode_basis, coef_table, table_index, wave_lengths, sed_table, template_ids):
    slabs, field_parts, group_parts = sizes
    count, rows, _ = mode_basis.shape
    fields, templates = template_ids.shape
    upix = PIX // slabs
    plane = field_parts * group_parts
    chips = plane // 2
    own = -(-count // plane)
    modes = plane * own

    coeffs = jnp.take(coef_table, table_index, axis=0, mode="clip")
    coeffs = jnp.pad(coeffs, ((0, 0), (0, modes - count)))
    same = jnp.eye(GROUP, dtype=jnp.bfloat16)
    mix = (coeffs[:, None, :, None] * same[None, :, None, :]).reshape(fields * GROUP, -1)
    raw = jnp.take(sed_table, template_ids, axis=0, mode="clip")
    weights = (raw / jnp.sum(raw, axis=2, keepdims=True)).astype(jnp.bfloat16).astype(jnp.float32)
    lengths = jnp.broadcast_to(wave_lengths[:, None, None], (wave_lengths.shape[0], 8, PUP))
    hops = slabs - 1
    dma = pltpu.SemaphoreType.DMA

    return pl.pallas_call(
        functools.partial(psf_kernel, sizes, waves, fields),
        in_specs=[
            pl.BlockSpec(memory_space=pltpu.VMEM),
            pl.BlockSpec(memory_space=pltpu.SMEM),
            pl.BlockSpec(memory_space=pltpu.VMEM),
            pl.BlockSpec(memory_space=pl.ANY),
        ],
        out_specs=pl.BlockSpec(memory_space=pltpu.VMEM),
        out_shape=jax.ShapeDtypeStruct((fields, templates, upix, PIX), jnp.bfloat16),
        scratch_shapes=[
            pltpu.VMEM((slabs, modes, rows, PUP), jnp.bfloat16),
            pltpu.VMEM((waves, 8, PUP), jnp.float32),
            pltpu.VMEM((fields, rows, PUP), jnp.float32),
            pltpu.VMEM((waves, fields * upix, 2 * PUP), jnp.float32),
            pltpu.VMEM((2 * PUP, 2 * PIX), jnp.bfloat16),
            pltpu.VMEM((2 * rows, PUP), jnp.bfloat16),
            pltpu.VMEM((2 * rows, PUP), jnp.bfloat16),
            pltpu.VMEM((rows, PUP), jnp.bfloat16),
            pltpu.VMEM((waves, fields * upix, PIX), jnp.float32),
            pltpu.VMEM((waves, fields, PIX), jnp.float32),
            pltpu.VMEM((hops, waves, fields, PIX), jnp.float32),
            dma,
            dma((hops,)),
            dma((hops,)),
            dma((hops,)),
            dma((hops,)),
            dma((hops, chips - 1)),
            dma((hops, chips - 1)),
            dma((hops,)),
            dma((hops,)),
            dma((hops,)),
            dma((hops,)),
        ],
        compiler_params=pltpu.CompilerParams(
            vmem_limit_bytes=60 * 2**20, collective_id=0, has_side_effects=True
        ),
    )(mix, weights.reshape(-1), lengths, mode_basis)


def solution(mesh):
    sizes = (mesh.shape["wave"], mesh.shape["field"], mesh.shape["groups"])


    def whole_program(*args):
        return sharded(mesh, functools.partial(local, sizes, args[3].shape[0]))(*args)

    return whole_program


def sharded(mesh, body):
    return jax.shard_map(
        body,
        mesh=mesh,
        in_specs=(
            P(None, "wave", None),
            P(),
            P(("groups", "field")),
            P("wave"),
            P(),
            P(("groups", "field"), None),
        ),
        out_specs=P(("groups", "field"), None, "wave", None),
        check_vma=False,
    )
```

profile of v0, /device:TPU:0, one launch (start us, length us, event | category | flops | bytes accessed | tf_op | source)
XLA Modules:
  0.0 135.1 jit_solution(13754452532910003498)
XLA Ops:
  0.0 0.8 reshape.33
  0.8 0.7 pad_clamp_fusion.1
  1.4 1.3 broadcast_in_dim.19.length_ref
  2.8 0.9 copy.10
  3.7 0.6 gather_fusion.1
  4.3 0.1 reduce.1
  4.4 0.1 reshape.42
  4.5 0.1 fusion.1
  4.6 0.7 reshape.22.weight_ref
  5.3 1.4 %copy.9 = bf16[4096,22]{1,0:T(8,128)(2,1)S(1)} copy(bf16[4096,22]{0,1:T(8,128)(2,1)} %param.7) | data formatting | bytes 360448 | tf_op args[1]
  6.7 0.6 gather_fusion
  7.3 0.1 broadcast_multiply_fusion
  7.4 1.2 mul.20.mix_ref
  8.6 123.3 %shard_map.64 = bf16[8,8,64,256]{3,2,1,0:T(8,128)(2,1)} custom-call(bf16[128,384]{1,0:T(8,128)(2,1)} %mul.20.mix_ref, f32[512]{0:T(512)} %reshape.22.weight_ref, f32[2,8,512]{2,1,0:T(8,128)} %broadcast_in_dim.19.length_ref, bf16[22,128,512]{2,1,0:T(8,128)(2,1)} %basis_ref.1), custom_call_target="tpu_custom_call" | custom-call | tf_op jit(solution)/shard_map/pallas_call | solution.py:365
  131.9 3.2 %copy.12 = bf16[8,8,64,256]{3,2,1,0:T(8,128)(2,1)} copy(bf16[8,8,64,256]{3,2,1,0:T(8,128)(2,1)} %shard_map.64) | data formatting | bytes 4194304
  (3 shorter events, 0.0 us)
where the time goes:
time: 135 us
  Pallas kernels  123 us (91%)
  local copies, waits for them, and re-layouts  10.7 us (8%)
    pallas_call x1, Pallas kernels, local(): pl.pallas_call(functools.partial(psf_kernel, sizes, waves, fields), in_sp...  123 us
    unnamed x3, local copies, waits for them, and re-layouts  5.53 us

commit v1 on v0

v1 whole, which is shorter than its diff:
```python
import functools

import jax
import jax.numpy as jnp
import numpy as np
from jax import lax
from jax.experimental import pallas as pl
from jax.experimental.pallas import tpu as pltpu
from jax.sharding import PartitionSpec as P

PUP = 512
PIX = 256
EPSILON = 1e-06
GROUP = 16
LANES = 128
CHUNKS = 2
ROUNDER = 12582912.0

SIN = (4.442879676818848, -7.307816505432129, 3.5977742671966553, -0.7911993861198425)
COS = (1.4142135381698608, -6.978850841522217, 5.739460468292236, -1.883557915687561, 0.3106880187988281)
SHORT_SIN = (4.440917015075684, -7.256804466247559, 3.229630470275879)
SHORT_COS = (1.414183259010315, -6.976953506469727, 5.709674835205078, -1.7155721187591553)


def horner(coefficients, s):
    value = coefficients[-1]
    for c in coefficients[-2::-1]:
        value = c + s * value
    return value


def turns_sincos(turns, sine=SIN, cosine=COS):
    nearest = (turns + ROUNDER) - ROUNDER
    r = turns - nearest
    s = r * r
    a = r * horner(sine, s)
    b = horner(cosine, s)
    return 1.0 - a * a, a * b


def packed_tiles(slabs, rows):
    pos = 2 * np.arange(PUP) - PUP + 1
    radius = pos[:, None] ** 2 + pos[None, :] ** 2
    inside = (radius <= PUP * PUP) & (radius >= (61 * PUP // 100) ** 2)
    columns = PUP // LANES
    half = LANES // 2
    result = []
    for slab in range(slabs):
        tiles = []
        for group in range(rows // GROUP):
            first = slab * rows + group * GROUP
            need = inside[first : first + GROUP].any(axis=0).reshape(columns, LANES)
            low, high = need[:, :half].any(axis=1), need[:, half:].any(axis=1)
            lows = [c for c in range(columns) if low[c] and not high[c]]
            highs = [c for c in range(columns) if high[c] and not low[c]]
            pairs = list(zip(lows, highs))
            for c in range(columns):
                if low[c] and high[c]:
                    tiles.append((group, (c,)))
            tiles += [(group, pair) for pair in pairs]
            tiles += [(group, (c,)) for c in lows[len(pairs) :] + highs[len(pairs) :]]
        result.append(tuple(tiles))
    return result


def hop(order, slabs):
    odd = order % 2
    return odd * ((order + 1) // 2) + (1 - odd) * (slabs - order // 2)


def psf_kernel(
    sizes, waves, fields, share, mix_ref, weight_ref, length_ref, basis_ref, out_ref,
    held, whole, inverse, path, image, tables, efield0, efield1, opening, power, total, arrived,
    local_sem, wl_send, wl_recv, send1, recv1, send2, recv2, send3, recv3, sum_send, sum_recv,
):
    slabs, field_parts, group_parts = sizes
    count, rows, _ = basis_ref.shape
    upix = PIX // slabs
    own_waves = waves // slabs
    x_parts = field_parts // 2
    chips = x_parts * group_parts
    templates = out_ref.shape[1]
    layout = packed_tiles(slabs, rows)
    kept_tables = tables.shape[0] == waves

    me = lax.axis_index("wave")
    part = lax.axis_index("field")
    core = part % 2
    chip = lax.axis_index("groups") * x_parts + part // 2
    first_pix = me * upix

    def wave_peer(shift):
        return {"wave": (me + shift) % slabs}

    def chip_device(other):
        return {"groups": other // x_parts, "field": (other % x_parts) * 2 + core}

    sibling = {"field": part + 1 - 2 * core}

    def remote(src, dst, send, recv, device):
        return pltpu.make_async_remote_copy(
            src_ref=src, dst_ref=dst, send_sem=send, recv_sem=recv,
            device_id=device, device_id_type=pl.DeviceIdType.MESH,
        )

    def from_slab(order):
        return (me + 2 * slabs - hop(order, slabs)) % slabs

    def block(slab, of_core, chunk, of_chip, pieces=1):
        first = ((of_core * CHUNKS + chunk) * chips + of_chip) * share
        return whole.at[slab, pl.ds(first, pieces * share)]

    def first_copy(order, chunk):
        ref = block(me, core, chunk, chip)
        at = (order - 1, chunk)
        return remote(ref, ref, send1.at[at], recv1.at[at], wave_peer(hop(order, slabs)))

    def first_landed(order, chunk):
        ref = block(from_slab(order), core, chunk, chip)
        at = (order - 1, chunk)
        return remote(ref, ref, send1.at[at], recv1.at[at], wave_peer(hop(order, slabs)))

    relay = x_parts == 2 and group_parts == 2
    chip_x, chip_y = chip % x_parts, chip // x_parts
    flip_x, flip_y = 1 - 2 * chip_x, 1 - 2 * chip_y
    first_chip = (chip_y + core * flip_y) * x_parts + chip_x + (1 - core) * flip_x
    second_chip = (chip_y + (1 - core) * flip_y) * x_parts + chip_x + core * flip_x

    def plane_copy(order, chunk, shift):
        at = (order - 1, chunk, shift - 1)
        slab = from_slab(order)
        if relay:
            ref = block(slab, core, chunk, first_chip if shift == 3 else chip)
            device = chip_device(first_chip if shift == 1 else second_chip)
        else:
            ref = block(slab, core, chunk, chip)
            device = chip_device((chip + shift) % chips)
        return remote(ref, ref, send2.at[at], recv2.at[at], device)

    def plane_landed(order, chunk, shift):
        at = (order - 1, chunk, shift - 1)
        if relay:
            sender = (first_chip, second_chip, chips - 1 - chip)[shift - 1]
        else:
            sender = (chip + chips - shift) % chips
        ref = block(from_slab(order), core, chunk, sender)
        return remote(ref, ref, send2.at[at], recv2.at[at], chip_device((chip + shift) % chips))

    def core_copy(order, chunk, which):
        ref = block(from_slab(order), which, chunk, 0, chips)
        at = (order - 1, chunk)
        return remote(ref, ref, send3.at[at], recv3.at[at], sibling)

    def length_copy(shift, sender):
        ref = inverse.at[pl.ds(sender * own_waves, own_waves)]
        return remote(ref, ref, wl_send.at[shift - 1], wl_recv.at[shift - 1], wave_peer(shift))

    barrier = pltpu.get_barrier_semaphore()
    peers = [wave_peer(d) for d in range(1, slabs)] + [chip_device((chip + e) % chips) for e in range(1, chips)] + [sibling]
    for peer in peers:
        pl.semaphore_signal(barrier, inc=1, device_id=peer, device_id_type=pl.DeviceIdType.MESH)
    bring = pltpu.make_async_copy(basis_ref, held, local_sem)
    bring.start()
    for i in range(own_waves):
        inverse[me * own_waves + i] = 1.0 / jnp.full(inverse.shape[1:], length_ref[i], jnp.float32)

    def clear(f, carry):
        for l in range(waves):
            image[l, pl.ds(f * upix, upix), :] = jnp.zeros((upix, 2 * PUP), jnp.float32)
        return carry

    lax.fori_loop(0, fields, clear, 0)
    bring.wait()

    low_lanes = (lax.broadcasted_iota(jnp.int32, (GROUP, LANES), 1) < LANES // 2).astype(jnp.float32)
    low_lanes, high_lanes = low_lanes.astype(jnp.bfloat16), (1.0 - low_lanes).astype(jnp.bfloat16)

    def pack(tiles, k, carry):
        for t, (group, columns) in enumerate(tiles):
            r = group * GROUP
            parts = [held[k, r : r + GROUP, c * LANES : (c + 1) * LANES] for c in columns]
            value = parts[0]
            if len(parts) == 2:
                value = parts[0] * low_lanes + parts[1] * high_lanes
            whole[me, t * count + k] = value
        return carry

    for slab, tiles in enumerate(layout):

        @pl.when(me == slab)
        def _():
            lax.fori_loop(0, count, functools.partial(pack, tiles), 0)

    pl.semaphore_wait(barrier, len(peers))
    for c in range(CHUNKS):
        first_copy(1, c).start()
    for d in range(1, slabs):
        length_copy(d, me).start()
    for d in range(1, slabs):
        length_copy(d, (me + slabs - d) % slabs).wait_recv()

    def second_table(wave, slot):
        scale = inverse[wave][:1, :PIX] * (0.25 / (2.0 * PUP))
        step = 64
        for r in range(0, PUP, step):
            ys = 2 * (r + lax.broadcasted_iota(jnp.int32, (step, PIX), 0)) - PUP + 1
            vs = lax.broadcasted_iota(jnp.int32, (step, PIX), 1) - PIX // 2
            cosine, sine = turns_sincos((ys * vs).astype(jnp.float32) * scale)
            cosine = cosine.astype(jnp.bfloat16)
            tables[slot, r : r + step, :PIX] = cosine
            tables[slot, r : r + step, PIX:] = (-sine).astype(jnp.bfloat16)
            tables[slot, PUP + r : PUP + r + step, :PIX] = sine.astype(jnp.bfloat16)
            tables[slot, PUP + r : PUP + r + step, PIX:] = cosine

    def at_eighth(order, eighths):
        return (order - 1) * waves + eighths * waves // 8

    def step_body(step, carry):
        order = step // waves
        wave = step % waves
        slab = from_slab(order)
        first_row = slab * rows

        if kept_tables:

            @pl.when(step == waves)
            def _():
                def make(l, c):
                    second_table(l, l)
                    return c

                lax.fori_loop(0, waves, make, 0)

        for o in range(1, slabs):
            for c in range(CHUNKS):

                @pl.when(step == at_eighth(o, 2 + 2 * c))
                def _():
                    first_landed(o, c).wait_recv()
                    for e in range(1, 3 if relay else chips):
                        plane_copy(o, c, e).start()
                    if o + 1 < slabs:
                        first_copy(o + 1, c).start()

                if relay:

                    @pl.when(step == at_eighth(o, 4 + 2 * c))
                    def _():
                        plane_landed(o, c, 1).wait_recv()
                        plane_copy(o, c, 3).start()

                @pl.when(step == at_eighth(o, 6 + 2 * c))
                def _():
                    for e in range(2 if relay else 1, chips):
                        plane_landed(o, c, e).wait_recv()
                    core_copy(o, c, core).start()

            @pl.when(step == o * waves)
            def _():
                for c in range(CHUNKS):
                    core_copy(o, c, 1 - core).wait_recv()

        @pl.when(wave == 0)
        def _():
            def paths(i, c):
                pair = [whole[slab, pl.ds((2 * i + b) * count, count)].reshape(count * GROUP, LANES) for b in range(2)]
                diff = jnp.dot(mix_ref[...], jnp.concatenate(pair, axis=1), preferred_element_type=jnp.float32)
                for b in range(2):
                    path[:, 2 * i + b] = diff[:, b * LANES : (b + 1) * LANES].reshape(fields, GROUP, LANES)
                return c

            def openings(g, c):
                r = pl.multiple_of(g * GROUP, GROUP)
                x = 2 * (first_row + r + lax.broadcasted_iota(jnp.int32, (GROUP, PUP), 0)) - PUP + 1
                y = 2 * lax.broadcasted_iota(jnp.int32, (GROUP, PUP), 1) - PUP + 1
                radius = x * x + y * y
                inner = 61 * PUP // 100
                inside = (radius <= PUP * PUP) & (radius >= inner * inner)
                opening[pl.ds(r, GROUP), :] = inside.astype(jnp.float32).astype(jnp.bfloat16)
                return c

            pairs = 0
            for s, tiles in enumerate(layout):
                pairs = jnp.where(slab == s, (len(tiles) + 1) // 2, pairs)
            lax.fori_loop(0, pairs, paths, 0)
            lax.fori_loop(0, rows // GROUP, openings, 0)
            for field in (efield0, efield1):
                field[...] = jnp.zeros_like(field)

        inv = inverse[wave]
        lane = lax.broadcasted_iota(jnp.int32, (upix, 2 * rows), 1)
        real = lane < rows
        xs = 2 * (first_row + jnp.where(real, lane, lane - rows)) - PUP + 1
        us = first_pix + lax.broadcasted_iota(jnp.int32, (upix, 2 * rows), 0) - PIX // 2
        scale = inv[:1, : 2 * rows] * (0.25 / (2.0 * PUP))
        cosine, sine = turns_sincos((us * xs).astype(jnp.float32) * scale)
        kernel = jnp.concatenate(
            [jnp.where(real, cosine, sine), jnp.where(real, -sine, cosine)], axis=0
        ).astype(jnp.bfloat16)
        tile = jnp.concatenate([inv[:, :LANES], inv[:, :LANES]], axis=0)

        def accumulate(f):
            field = (efield0, efield1)[f % 2]
            part_sum = jnp.dot(kernel, field[...], preferred_element_type=jnp.float32)
            here = pl.ds(f * upix, upix)
            image[wave, here, :PUP] += part_sum[:upix]
            image[wave, here, PUP:] += part_sum[upix:]

        def units(tiles):
            for f in range(fields):
                field = (efield0, efield1)[f % 2]
                for t, (group, columns) in enumerate(tiles):
                    r = group * GROUP
                    cosine, sine = turns_sincos(path[f, t] * tile, SHORT_SIN, SHORT_COS)
                    cosine, sine = cosine.astype(jnp.bfloat16), sine.astype(jnp.bfloat16)
                    for c in columns:
                        lanes = slice(c * LANES, (c + 1) * LANES)
                        hole = opening[r : r + GROUP, lanes]
                        field[r : r + GROUP, lanes] = cosine * hole
                        field[rows + r : rows + r + GROUP, lanes] = sine * hole
                if f > 0:
                    accumulate(f - 1)
            accumulate(fields - 1)

        for s, tiles in enumerate(layout):
            pl.when(slab == s)(functools.partial(units, tiles))

        return carry

    lax.fori_loop(0, slabs * waves, step_body, 0)

    def finish(wave, carry):
        if not kept_tables:
            second_table(wave, 0)
        slot = wave if kept_tables else 0
        half = fields * upix // 2
        for h in range(2):
            field = jnp.dot(
                image[wave, h * half : (h + 1) * half, :].astype(jnp.bfloat16),
                tables[slot],
                preferred_element_type=jnp.float32,
            )
            re, im = field[:, :PIX], field[:, PIX:]
            bright = re * re + im * im
            power[wave, h * half : (h + 1) * half, :] = bright
            sums = jnp.sum(jnp.sum(bright.reshape(fields // 2, upix, PIX), axis=1), axis=1, keepdims=True)
            total[wave, h * (fields // 2) : (h + 1) * (fields // 2), :] = jnp.broadcast_to(
                sums, (fields // 2, PIX)
            )
        return carry

    lax.fori_loop(0, waves, finish, 0)

    def sum_copy(shift):
        return remote(
            total, arrived.at[shift - 1], sum_send.at[shift - 1], sum_recv.at[shift - 1], wave_peer(shift)
        )

    for d in range(1, slabs):
        sum_copy(d).start()
    for d in range(1, slabs):
        sum_copy(d).wait()
    everything = total[...]
    for d in range(1, slabs):
        everything = everything + arrived[d - 1]
    total[...] = 1.0 / (everything * (1.0 / (PIX * PIX)) + EPSILON)

    step = 16

    def mix_fields(f, carry):
        for r in range(0, upix, step):
            sums = [None] * templates
            for l in range(waves):
                level = total[l, pl.ds(f, 1), :]
                bright = power[l, pl.ds(pl.multiple_of(f * upix, step) + r, step), :]
                spectrum = (bright * level).astype(jnp.bfloat16).astype(jnp.float32)
                for j in range(templates):
                    term = spectrum * weight_ref[(f * templates + j) * waves + l]
                    sums[j] = term if l == 0 else sums[j] + term
            for j in range(templates):
                out_ref[f, j, r : r + step, :] = sums[j].astype(jnp.bfloat16)
        return carry

    lax.fori_loop(0, fields, mix_fields, 0)

    for d in range(1, slabs):
        length_copy(d, me).wait_send()
    for o in range(1, slabs):
        for c in range(CHUNKS):
            first_copy(o, c).wait_send()
            for e in range(1, chips):
                plane_copy(o, c, e).wait_send()
            core_copy(o, c, core).wait_send()


def local(sizes, waves, mode_basis, coef_table, table_index, wave_lengths, sed_table, template_ids):
    slabs, field_parts, group_parts = sizes
    count, rows, _ = mode_basis.shape
    fields, templates = template_ids.shape
    upix = PIX // slabs
    chips = field_parts * group_parts // 2
    tiles = max(len(t) for t in packed_tiles(slabs, rows))
    share = -(-tiles * count // (2 * CHUNKS * chips))
    even = tiles + tiles % 2
    units = max(share * 2 * CHUNKS * chips, even * count)

    coeffs = jnp.take(coef_table, table_index, axis=0, mode="clip")
    same = jnp.eye(GROUP, dtype=jnp.bfloat16)
    mix = (coeffs[:, None, :, None] * same[None, :, None, :]).reshape(fields * GROUP, -1)
    raw = jnp.take(sed_table, template_ids, axis=0, mode="clip")
    weights = (raw / jnp.sum(raw, axis=2, keepdims=True)).astype(jnp.bfloat16).astype(jnp.float32)
    hops = slabs - 1
    dma = pltpu.SemaphoreType.DMA

    return pl.pallas_call(
        functools.partial(psf_kernel, sizes, waves, fields, share),
        in_specs=[
            pl.BlockSpec(memory_space=pltpu.VMEM),
            pl.BlockSpec(memory_space=pltpu.SMEM),
            pl.BlockSpec(memory_space=pltpu.SMEM),
            pl.BlockSpec(memory_space=pl.ANY),
        ],
        out_specs=pl.BlockSpec(memory_space=pltpu.VMEM),
        out_shape=jax.ShapeDtypeStruct((fields, templates, upix, PIX), jnp.bfloat16),
        scratch_shapes=[
            pltpu.VMEM((count, rows, PUP), jnp.bfloat16),
            pltpu.VMEM((slabs, units, GROUP, LANES), jnp.bfloat16),
            pltpu.VMEM((waves, 8, max(2 * rows, PIX)), jnp.float32),
            pltpu.VMEM((fields, even, GROUP, LANES), jnp.float32),
            pltpu.VMEM((waves, fields * upix, 2 * PUP), jnp.float32),
            pltpu.VMEM((waves if waves <= 8 else 1, 2 * PUP, 2 * PIX), jnp.bfloat16),
            pltpu.VMEM((2 * rows, PUP), jnp.bfloat16),
            pltpu.VMEM((2 * rows, PUP), jnp.bfloat16),
            pltpu.VMEM((rows, PUP), jnp.bfloat16),
            pltpu.VMEM((waves, fields * upix, PIX), jnp.float32),
            pltpu.VMEM((waves, fields, PIX), jnp.float32),
            pltpu.VMEM((hops, waves, fields, PIX), jnp.float32),
            dma,
            dma((hops,)),
            dma((hops,)),
            dma((hops, CHUNKS)),
            dma((hops, CHUNKS)),
            dma((hops, CHUNKS, chips - 1)),
            dma((hops, CHUNKS, chips - 1)),
            dma((hops, CHUNKS)),
            dma((hops, CHUNKS)),
            dma((hops,)),
            dma((hops,)),
        ],
        compiler_params=pltpu.CompilerParams(
            vmem_limit_bytes=60 * 2**20, collective_id=0, has_side_effects=True
        ),
    )(mix, weights.reshape(-1), wave_lengths, mode_basis)


def solution(mesh):
    sizes = (mesh.shape["wave"], mesh.shape["field"], mesh.shape["groups"])


    def whole_program(*args):
        return sharded(mesh, functools.partial(local, sizes, args[3].shape[0]))(*args)

    return whole_program


def sharded(mesh, body):
    return jax.shard_map(
        body,
        mesh=mesh,
        in_specs=(
            P(None, "wave", None),
            P(),
            P(("groups", "field")),
            P("wave"),
            P(),
            P(("groups", "field"), None),
        ),
        out_specs=P(("groups", "field"), None, "wave", None),
        check_vma=False,
    )
```

time: 135 us -> 133 us (0.985)
    pallas_call x1, Pallas kernels: 123 us -> 122 us  [local(): pl.pallas_call(functools.partial(psf_kernel, sizes, waves, fields, share)...]
where the time goes in v1:
time: 133 us; the launch traced here: 132 us
  Pallas kernels  122 us (92%)
  local copies, waits for them, and re-layouts  9.54 us (7%)
    pallas_call x1, Pallas kernels, local(): pl.pallas_call(functools.partial(psf_kernel, sizes, waves, fields, share)...  122 us
    unnamed x3, local copies, waits for them, and re-layouts  5.54 us

profile of v1, /device:TPU:0, one launch (start us, length us, event | category | flops | bytes accessed | tf_op | source)
XLA Modules:
  0.0 132.5 jit_solution(13072685070659922659)
XLA Ops:
  0.0 0.8 reshape.32
  0.8 0.7 pad_clamp_fusion.1
  1.4 1.0 copy.11
  2.4 0.6 gather_fusion.1
  3.0 0.1 reduce.1
  3.1 0.1 reshape.41
  3.2 0.1 fusion.1
  3.3 0.7 reshape.21.weight_ref
  4.0 1.4 %copy.9 = bf16[4096,22]{1,0:T(8,128)(2,1)S(1)} copy(bf16[4096,22]{0,1:T(8,128)(2,1)} %param.7) | data formatting | bytes 360448 | tf_op args[1]
  5.4 0.6 gather_fusion
  6.0 0.1 copy.10
  6.1 0.1 broadcast_multiply_fusion
  6.2 0.5 mul.20
  6.7 0.8 copy.12.mix_ref
  7.4 121.9 %shard_map.64 = bf16[8,8,64,256]{3,2,1,0:T(8,128)(2,1)} custom-call(bf16[128,352]{1,0:T(8,128)(2,1)} %copy.12.mix_ref, f32[512]{0:T(512)} %reshape.21.weight_ref, f32[2]{0:T(128)} %length_ref.1, bf16[22,128,512]{2,1,0:T(8,128)(2,1)} %basis_ref.1), custom_call_target="tpu_custom_call" | custom-call | tf_op jit(solution)/shard_map/pallas_call | solution.py:415
  129.3 3.2 %copy.14 = bf16[8,8,64,256]{3,2,1,0:T(8,128)(2,1)} copy(bf16[8,8,64,256]{3,2,1,0:T(8,128)(2,1)} %shard_map.64) | data formatting | bytes 4194304
  (2 shorter events, 0.0 us)

commit v2 on v1

--- a/solution.py
+++ b/solution.py
@@ -68,15 +68,41 @@
     return odd * ((order + 1) // 2) + (1 - odd) * (slabs - order // 2)
 
 
+def events_of(slabs):
+    timed = []
+    for order in range(1, slabs):
+        for chunk in range(CHUNKS):
+            q = (order - 1) * CHUNKS + chunk
+            timed += [(3 * q, (1, order, chunk)), (3 * q + 4, (2, order, chunk)), (3 * q + 6.5, (3, order, chunk))]
+        timed.append((3 * q + 6.75, (4, order, 0)))
+    return [event for _, event in sorted(timed)]
+
+
+def scheduled_events(slabs, waves):
+    plan, pending, reached = {}, [], 0
+    for event in events_of(slabs):
+        pending.append(event)
+        if event[0] == 4:
+            start = reached * waves
+            for i, early in enumerate(pending):
+                step = start + waves * (i + 1) // len(pending)
+                if reached == 0:
+                    step = 5 * waves // 8 if i == 0 else waves
+                plan.setdefault(step if early[0] != 4 else (reached + 1) * waves, []).append(early)
+            pending, reached = [], event[1]
+    return plan
+
+
 def psf_kernel(
     sizes, waves, fields, share, mix_ref, weight_ref, length_ref, basis_ref, out_ref,
-    held, whole, inverse, path, image, tables, efield0, efield1, opening, power, total, arrived,
-    local_sem, wl_send, wl_recv, send1, recv1, send2, recv2, send3, recv3, sum_send, sum_recv,
+    held, whole, inverse, path, image, tables, xtables, efield0, efield1, opening, power, total, arrived, staged,
+    local_sem, wl_send, wl_recv, send1, recv1, send2, recv2, send3, recv3, sum_send, sum_recv, out_send, out_recv,
 ):
     slabs, field_parts, group_parts = sizes
     count, rows, _ = basis_ref.shape
-    upix = PIX // slabs
+    upix = 2 * PIX // slabs
     own_waves = waves // slabs
+    pairs = slabs // 2
     x_parts = field_parts // 2
     chips = x_parts * group_parts
     templates = out_ref.shape[1]
@@ -87,7 +113,9 @@
     part = lax.axis_index("field")
     core = part % 2
     chip = lax.axis_index("groups") * x_parts + part // 2
-    first_pix = me * upix
+    side = me % 2
+    first_pix = (me // 2) * upix
+    partner = {"wave": me + 1 - 2 * side}
 
     def wave_peer(shift):
         return {"wave": (me + shift) % slabs}
@@ -212,14 +240,95 @@
             tables[slot, PUP + r : PUP + r + step, :PIX] = sine.astype(jnp.bfloat16)
             tables[slot, PUP + r : PUP + r + step, PIX:] = cosine
 
-    def at_eighth(order, eighths):
-        return (order - 1) * waves + eighths * waves // 8
+    def x_table(slab, wave):
+        lane = lax.broadcasted_iota(jnp.int32, (upix, 2 * rows), 1)
+        real = lane < rows
+        xs = 2 * (slab * rows + jnp.where(real, lane, lane - rows)) - PUP + 1
+        us = first_pix + lax.broadcasted_iota(jnp.int32, (upix, 2 * rows), 0) - PIX // 2
+        scale = inverse[wave][:1, : 2 * rows] * (0.25 / (2.0 * PUP))
+        cosine, sine = turns_sincos((us * xs).astype(jnp.float32) * scale)
+        return jnp.concatenate(
+            [jnp.where(real, cosine, sine), jnp.where(real, -sine, cosine)], axis=0
+        ).astype(jnp.bfloat16)
+
+    def open_slab(slab):
+        def openings(g, c):
+            r = pl.multiple_of(g * GROUP, GROUP)
+            x = 2 * (slab * rows + r + lax.broadcasted_iota(jnp.int32, (GROUP, PUP), 0)) - PUP + 1
+            y = 2 * lax.broadcasted_iota(jnp.int32, (GROUP, PUP), 1) - PUP + 1
+            radius = x * x + y * y
+            inner = 61 * PUP // 100
+            inside = (radius <= PUP * PUP) & (radius >= inner * inner)
+            opening[pl.ds(r, GROUP), :] = inside.astype(jnp.float32).astype(jnp.bfloat16)
+            return c
+
+        lax.fori_loop(0, rows // GROUP, openings, 0)
+        for field in (efield0, efield1):
+            field[...] = jnp.zeros_like(field)
+
+    def slab_paths(slab):
+        mix = mix_ref[pl.ds(pl.multiple_of(side * fields * GROUP, GROUP), fields * GROUP), :]
+
+        def paths(i, c):
+            pair = [whole[slab, pl.ds((2 * i + b) * count, count)].reshape(count * GROUP, LANES) for b in range(2)]
+            diff = jnp.dot(mix, jnp.concatenate(pair, axis=1), preferred_element_type=jnp.float32)
+            for b in range(2):
+                path[:, 2 * i + b] = diff[:, b * LANES : (b + 1) * LANES].reshape(fields, GROUP, LANES)
+            return c
+
+        tile_pairs = 0
+        for number, tiles in enumerate(layout):
+            tile_pairs = jnp.where(slab == number, (len(tiles) + 1) // 2, tile_pairs)
+        lax.fori_loop(0, tile_pairs, paths, 0)
+
+    def fill(field, tiles, f, inv):
+        for t, (group, columns) in enumerate(tiles):
+            r = group * GROUP
+            cosine, sine = turns_sincos(path[f, t] * inv, SHORT_SIN, SHORT_COS)
+            cosine, sine = cosine.astype(jnp.bfloat16), sine.astype(jnp.bfloat16)
+            for c in columns:
+                lanes = slice(c * LANES, (c + 1) * LANES)
+                hole = opening[r : r + GROUP, lanes]
+                field[r : r + GROUP, lanes] = cosine * hole
+                field[rows + r : rows + r + GROUP, lanes] = sine * hole
+
+    def inverse_tile(wave):
+        inv = inverse[wave]
+        return jnp.concatenate([inv[:, :LANES], inv[:, :LANES]], axis=0)
+
+    def accumulate(kernel, field, wave, f):
+        part_sum = jnp.dot(kernel, field[...], preferred_element_type=jnp.float32)
+        here = pl.ds(f * upix, upix)
+        image[wave, here, :PUP] += part_sum[:upix]
+        image[wave, here, PUP:] += part_sum[upix:]
+
+    def handle(event):
+        stage, o, c = event
+        if stage == 1:
+            first_landed(o, c).wait_recv()
+            for e in range(1, 3 if relay else chips):
+                plane_copy(o, c, e).start()
+            if o + 1 < slabs:
+                first_copy(o + 1, c).start()
+        if stage == 2 and relay:
+            plane_landed(o, c, 1).wait_recv()
+            plane_copy(o, c, 3).start()
+        if stage == 3:
+            for e in range(2 if relay else 1, chips):
+                plane_landed(o, c, e).wait_recv()
+            core_copy(o, c, core).start()
+        if stage == 4:
+            for each in range(CHUNKS):
+                core_copy(o, each, 1 - core).wait_recv()
+
+    efields = (efield0, efield1)
+    plan = scheduled_events(slabs, waves)
+    last_step = (slabs - 1) * waves
 
     def step_body(step, carry):
         order = step // waves
         wave = step % waves
         slab = from_slab(order)
-        first_row = slab * rows
 
         if kept_tables:
 
@@ -231,157 +340,146 @@
 
                 lax.fori_loop(0, waves, make, 0)
 
-        for o in range(1, slabs):
-            for c in range(CHUNKS):
-
-                @pl.when(step == at_eighth(o, 2 + 2 * c))
+        for at, events in plan.items():
+            if at < last_step:
+
+                @pl.when(step == at)
                 def _():
-                    first_landed(o, c).wait_recv()
-                    for e in range(1, 3 if relay else chips):
-                        plane_copy(o, c, e).start()
-                    if o + 1 < slabs:
-                        first_copy(o + 1, c).start()
-
-                if relay:
-
-                    @pl.when(step == at_eighth(o, 4 + 2 * c))
-                    def _():
-                        plane_landed(o, c, 1).wait_recv()
-                        plane_copy(o, c, 3).start()
-
-                @pl.when(step == at_eighth(o, 6 + 2 * c))
-                def _():
-                    for e in range(2 if relay else 1, chips):
-                        plane_landed(o, c, e).wait_recv()
-                    core_copy(o, c, core).start()
-
-            @pl.when(step == o * waves)
-            def _():
-                for c in range(CHUNKS):
-                    core_copy(o, c, 1 - core).wait_recv()
+                    for event in events:
+                        handle(event)
 
         @pl.when(wave == 0)
         def _():
-            def paths(i, c):
-                pair = [whole[slab, pl.ds((2 * i + b) * count, count)].reshape(count * GROUP, LANES) for b in range(2)]
-                diff = jnp.dot(mix_ref[...], jnp.concatenate(pair, axis=1), preferred_element_type=jnp.float32)
-                for b in range(2):
-                    path[:, 2 * i + b] = diff[:, b * LANES : (b + 1) * LANES].reshape(fields, GROUP, LANES)
-                return c
-
-            def openings(g, c):
-                r = pl.multiple_of(g * GROUP, GROUP)
-                x = 2 * (first_row + r + lax.broadcasted_iota(jnp.int32, (GROUP, PUP), 0)) - PUP + 1
-                y = 2 * lax.broadcasted_iota(jnp.int32, (GROUP, PUP), 1) - PUP + 1
-                radius = x * x + y * y
-                inner = 61 * PUP // 100
-                inside = (radius <= PUP * PUP) & (radius >= inner * inner)
-                opening[pl.ds(r, GROUP), :] = inside.astype(jnp.float32).astype(jnp.bfloat16)
-                return c
-
-            pairs = 0
-            for s, tiles in enumerate(layout):
-                pairs = jnp.where(slab == s, (len(tiles) + 1) // 2, pairs)
-            lax.fori_loop(0, pairs, paths, 0)
-            lax.fori_loop(0, rows // GROUP, openings, 0)
-            for field in (efield0, efield1):
-                field[...] = jnp.zeros_like(field)
-
-        inv = inverse[wave]
-        lane = lax.broadcasted_iota(jnp.int32, (upix, 2 * rows), 1)
-        real = lane < rows
-        xs = 2 * (first_row + jnp.where(real, lane, lane - rows)) - PUP + 1
-        us = first_pix + lax.broadcasted_iota(jnp.int32, (upix, 2 * rows), 0) - PIX // 2
-        scale = inv[:1, : 2 * rows] * (0.25 / (2.0 * PUP))
-        cosine, sine = turns_sincos((us * xs).astype(jnp.float32) * scale)
-        kernel = jnp.concatenate(
-            [jnp.where(real, cosine, sine), jnp.where(real, -sine, cosine)], axis=0
-        ).astype(jnp.bfloat16)
-        tile = jnp.concatenate([inv[:, :LANES], inv[:, :LANES]], axis=0)
-
-        def accumulate(f):
-            field = (efield0, efield1)[f % 2]
-            part_sum = jnp.dot(kernel, field[...], preferred_element_type=jnp.float32)
-            here = pl.ds(f * upix, upix)
-            image[wave, here, :PUP] += part_sum[:upix]
-            image[wave, here, PUP:] += part_sum[upix:]
+            slab_paths(slab)
+            open_slab(slab)
+
+        kernel = x_table(slab, wave)
+        inv = inverse_tile(wave)
 
         def units(tiles):
             for f in range(fields):
-                field = (efield0, efield1)[f % 2]
-                for t, (group, columns) in enumerate(tiles):
-                    r = group * GROUP
-                    cosine, sine = turns_sincos(path[f, t] * tile, SHORT_SIN, SHORT_COS)
-                    cosine, sine = cosine.astype(jnp.bfloat16), sine.astype(jnp.bfloat16)
-                    for c in columns:
-                        lanes = slice(c * LANES, (c + 1) * LANES)
-                        hole = opening[r : r + GROUP, lanes]
-                        field[r : r + GROUP, lanes] = cosine * hole
-                        field[rows + r : rows + r + GROUP, lanes] = sine * hole
+                fill(efields[f % 2], tiles, f, inv)
                 if f > 0:
-                    accumulate(f - 1)
-            accumulate(fields - 1)
-
-        for s, tiles in enumerate(layout):
-            pl.when(slab == s)(functools.partial(units, tiles))
+                    accumulate(kernel, efields[(f - 1) % 2], wave, f - 1)
+            accumulate(kernel, efields[(fields - 1) % 2], wave, fields - 1)
+
+        for number, tiles in enumerate(layout):
+            pl.when(slab == number)(functools.partial(units, tiles))
 
         return carry
 
-    lax.fori_loop(0, slabs * waves, step_body, 0)
-
-    def finish(wave, carry):
-        if not kept_tables:
-            second_table(wave, 0)
-        slot = wave if kept_tables else 0
-        half = fields * upix // 2
-        for h in range(2):
+    lax.fori_loop(0, last_step, step_body, 0)
+
+    last = from_slab(slabs - 1)
+
+    def make_x(l, c):
+        xtables[l] = x_table(last, l)
+        return c
+
+    lax.fori_loop(0, waves, make_x, 0)
+    open_slab(last)
+    for event in plan[last_step]:
+        handle(event)
+    slab_paths(last)
+
+    def sum_copy(f, shift):
+        at = (f, shift - 1)
+        return remote(
+            total.at[f], arrived.at[shift - 1, f], sum_send.at[at], sum_recv.at[at], {"wave": (me + 2 * shift) % slabs}
+        )
+
+    def out_copy(f):
+        return remote(staged.at[f], out_ref.at[side * fields + f], out_send.at[f], out_recv.at[f], partner)
+
+    def out_landed(f):
+        ref = out_ref.at[(1 - side) * fields + f]
+        return remote(ref, ref, out_send.at[f], out_recv.at[f], partner)
+
+    def last_fields(f):
+        def two_waves(i, c):
+            def units(tiles):
+                for b in range(2):
+                    fill(efields[b], tiles, f, inverse_tile(2 * i + b))
+                    if b > 0:
+                        accumulate(xtables[2 * i], efield0, 2 * i, f)
+                accumulate(xtables[2 * i + 1], efield1, 2 * i + 1, f)
+
+            for number, tiles in enumerate(layout):
+                pl.when(last == number)(functools.partial(units, tiles))
+            return c
+
+        lax.fori_loop(0, waves // 2, two_waves, 0)
+
+        def finish(wave, c):
+            if not kept_tables:
+                second_table(wave, 0)
+            here = pl.ds(pl.multiple_of(f * upix, GROUP), upix)
             field = jnp.dot(
-                image[wave, h * half : (h + 1) * half, :].astype(jnp.bfloat16),
-                tables[slot],
+                image[wave, here, :].astype(jnp.bfloat16),
+                tables[wave if kept_tables else 0],
                 preferred_element_type=jnp.float32,
             )
             re, im = field[:, :PIX], field[:, PIX:]
             bright = re * re + im * im
-            power[wave, h * half : (h + 1) * half, :] = bright
-            sums = jnp.sum(jnp.sum(bright.reshape(fields // 2, upix, PIX), axis=1), axis=1, keepdims=True)
-            total[wave, h * (fields // 2) : (h + 1) * (fields // 2), :] = jnp.broadcast_to(
-                sums, (fields // 2, PIX)
+            power[wave, here, :] = bright
+            total[f, pl.ds(wave, 1), :] = jnp.broadcast_to(
+                jnp.sum(jnp.sum(bright, axis=0, keepdims=True), axis=1, keepdims=True), (1, PIX)
             )
+            return c
+
+        lax.fori_loop(0, waves, finish, 0)
+        for d in range(1, pairs):
+            sum_copy(f, d).start()
+
+    def mix_field(f):
+        everything = total[f]
+        for d in range(1, pairs):
+            sum_copy(f, d).wait()
+            everything = everything + arrived[d - 1, f]
+        level_all = 1.0 / (everything * (1.0 / (PIX * PIX)) + EPSILON)
+        levels = [level_all[l : l + 1, :] for l in range(waves)]
+        step = 16
+
+        def rows_of(first, store):
+            def chunk(i, c):
+                r = pl.multiple_of(i * step, step)
+                sums = [None] * templates
+                for l in range(waves):
+                    bright = power[l, pl.ds(pl.multiple_of(f * upix + first, step) + r, step), :]
+                    spectrum = (bright * levels[l]).astype(jnp.bfloat16).astype(jnp.float32)
+                    for j in range(templates):
+                        term = spectrum * weight_ref[((side * fields + f) * templates + j) * waves + l]
+                        sums[j] = term if l == 0 else sums[j] + term
+                for j in range(templates):
+                    store(j, r, sums[j].astype(jnp.bfloat16))
+                return c
+
+            lax.fori_loop(0, upix // 2 // step, chunk, 0)
+
+        def to_partner(j, r, value):
+            staged[f, j, pl.ds(r, step), :] = value
+
+        def to_own(j, r, value):
+            out_ref[side * fields + f, j, pl.ds(r, step), :] = value
+
+        rows_of((1 - side) * (upix // 2), to_partner)
+        out_copy(f).start()
+        rows_of(side * (upix // 2), to_own)
+
+    def tail(f, carry):
+        last_fields(f)
+
+        @pl.when(f > 0)
+        def _():
+            mix_field(f - 1)
+
         return carry
 
-    lax.fori_loop(0, waves, finish, 0)
-
-    def sum_copy(shift):
-        return remote(
-            total, arrived.at[shift - 1], sum_send.at[shift - 1], sum_recv.at[shift - 1], wave_peer(shift)
-        )
-
-    for d in range(1, slabs):
-        sum_copy(d).start()
-    for d in range(1, slabs):
-        sum_copy(d).wait()
-    everything = total[...]
-    for d in range(1, slabs):
-        everything = everything + arrived[d - 1]
-    total[...] = 1.0 / (everything * (1.0 / (PIX * PIX)) + EPSILON)
-
-    step = 16
-
-    def mix_fields(f, carry):
-        for r in range(0, upix, step):
-            sums = [None] * templates
-            for l in range(waves):
-                level = total[l, pl.ds(f, 1), :]
-                bright = power[l, pl.ds(pl.multiple_of(f * upix, step) + r, step), :]
-                spectrum = (bright * level).astype(jnp.bfloat16).astype(jnp.float32)
-                for j in range(templates):
-                    term = spectrum * weight_ref[(f * templates + j) * waves + l]
-                    sums[j] = term if l == 0 else sums[j] + term
-            for j in range(templates):
-                out_ref[f, j, r : r + step, :] = sums[j].astype(jnp.bfloat16)
-        return carry
-
-    lax.fori_loop(0, fields, mix_fields, 0)
+    lax.fori_loop(0, fields, tail, 0)
+    mix_field(fields - 1)
+    for f in range(fields):
+        out_landed(f).wait_recv()
+        out_copy(f).wait_send()
 
     for d in range(1, slabs):
         length_copy(d, me).wait_send()
@@ -397,7 +495,8 @@
     slabs, field_parts, group_parts = sizes
     count, rows, _ = mode_basis.shape
     fields, templates = template_ids.shape
-    upix = PIX // slabs
+    upix = 2 * PIX // slabs
+    half = fields // 2
     chips = field_parts * group_parts // 2
     tiles = max(len(t) for t in packed_tiles(slabs, rows))
     share = -(-tiles * count // (2 * CHUNKS * chips))
@@ -410,10 +509,11 @@
     raw = jnp.take(sed_table, template_ids, axis=0, mode="clip")
     weights = (raw / jnp.sum(raw, axis=2, keepdims=True)).astype(jnp.bfloat16).astype(jnp.float32)
     hops = slabs - 1
+    others = slabs // 2 - 1
     dma = pltpu.SemaphoreType.DMA
 
     return pl.pallas_call(
-        functools.partial(psf_kernel, sizes, waves, fields, share),
+        functools.partial(psf_kernel, sizes, waves, half, share),
         in_specs=[
             pl.BlockSpec(memory_space=pltpu.VMEM),
             pl.BlockSpec(memory_space=pltpu.SMEM),
@@ -421,20 +521,22 @@
             pl.BlockSpec(memory_space=pl.ANY),
         ],
         out_specs=pl.BlockSpec(memory_space=pltpu.VMEM),
-        out_shape=jax.ShapeDtypeStruct((fields, templates, upix, PIX), jnp.bfloat16),
+        out_shape=jax.ShapeDtypeStruct((fields, templates, upix // 2, PIX), jnp.bfloat16),
         scratch_shapes=[
             pltpu.VMEM((count, rows, PUP), jnp.bfloat16),
             pltpu.VMEM((slabs, units, GROUP, LANES), jnp.bfloat16),
             pltpu.VMEM((waves, 8, max(2 * rows, PIX)), jnp.float32),
-            pltpu.VMEM((fields, even, GROUP, LANES), jnp.float32),
-            pltpu.VMEM((waves, fields * upix, 2 * PUP), jnp.float32),
+            pltpu.VMEM((half, even, GROUP, LANES), jnp.float32),
+            pltpu.VMEM((waves, half * upix, 2 * PUP), jnp.float32),
             pltpu.VMEM((waves if waves <= 8 else 1, 2 * PUP, 2 * PIX), jnp.bfloat16),
+            pltpu.VMEM((waves, 2 * upix, 2 * rows), jnp.bfloat16),
             pltpu.VMEM((2 * rows, PUP), jnp.bfloat16),
             pltpu.VMEM((2 * rows, PUP), jnp.bfloat16),
             pltpu.VMEM((rows, PUP), jnp.bfloat16),
-            pltpu.VMEM((waves, fields * upix, PIX), jnp.float32),
-            pltpu.VMEM((waves, fields, PIX), jnp.float32),
-            pltpu.VMEM((hops, waves, fields, PIX), jnp.float32),
+            pltpu.VMEM((waves, half * upix, PIX), jnp.float32),
+            pltpu.VMEM((half, waves, PIX), jnp.float32),
+            pltpu.VMEM((others, half, waves, PIX), jnp.float32),
+            pltpu.VMEM((half, templates, upix // 2, PIX), jnp.bfloat16),
             dma,
             dma((hops,)),
             dma((hops,)),
@@ -444,8 +546,10 @@
             dma((hops, CHUNKS, chips - 1)),
             dma((hops, CHUNKS)),
             dma((hops, CHUNKS)),
-            dma((hops,)),
-            dma((hops,)),
+            dma((half, others)),
+            dma((half, others)),
+            dma((half,)),
+            dma((half,)),
         ],
         compiler_params=pltpu.CompilerParams(
             vmem_limit_bytes=60 * 2**20, collective_id=0, has_side_effects=True

time: 133 us -> 132 us (level)
  no operation moved by 1% of the time
where the time goes in v2:
time: 132 us
  Pallas kernels  121 us (92%)
  local copies, waits for them, and re-layouts  9.54 us (7%)
    pallas_call x1, Pallas kernels, local(): pl.pallas_call(functools.partial(psf_kernel, sizes, waves, half, share),...  121 us
    unnamed x3, local copies, waits for them, and re-layouts  5.54 us

profile of v2, /device:TPU:0, one launch (start us, length us, event | category | flops | bytes accessed | tf_op | source)
XLA Modules:
  0.0 132.0 jit_solution(3391810297438811149)
XLA Ops:
  0.0 0.8 reshape.32
  0.8 0.7 pad_clamp_fusion.1
  1.4 1.0 copy.11
  2.4 0.6 gather_fusion.1
  3.0 0.1 reduce.1
  3.1 0.1 reshape.41
  3.2 0.1 fusion.1
  3.3 0.7 reshape.21.weight_ref
  4.0 1.4 %copy.9 = bf16[4096,22]{1,0:T(8,128)(2,1)S(1)} copy(bf16[4096,22]{0,1:T(8,128)(2,1)} %param.7) | data formatting | bytes 360448 | tf_op args[1]
  5.4 0.6 gather_fusion
  6.0 0.1 copy.10
  6.1 0.1 broadcast_multiply_fusion
  6.2 0.5 mul.20
  6.7 0.8 copy.12.mix_ref
  7.4 121.5 %shard_map.64 = bf16[8,8,64,256]{3,2,1,0:T(8,128)(2,1)} custom-call(bf16[128,352]{1,0:T(8,128)(2,1)} %copy.12.mix_ref, f32[512]{0:T(512)} %reshape.21.weight_ref, f32[2]{0:T(128)} %length_ref.1, bf16[22,128,512]{2,1,0:T(8,128)(2,1)} %basis_ref.1), custom_call_target="tpu_custom_call" | custom-call | tf_op jit(solution)/shard_map/pallas_call | solution.py:515
  128.9 3.2 %copy.14 = bf16[8,8,64,256]{3,2,1,0:T(8,128)(2,1)} copy(bf16[8,8,64,256]{3,2,1,0:T(8,128)(2,1)} %shard_map.64) | data formatting | bytes 4194304
  (2 shorter events, 0.0 us)

commit v3 on v2

--- a/solution.py
+++ b/solution.py
@@ -13,7 +13,10 @@
 EPSILON = 1e-06
 GROUP = 16
 LANES = 128
+WIDE = 256
 CHUNKS = 2
+AHEAD = 4
+BATCH = 6
 ROUNDER = 12582912.0
 
 SIN = (4.442879676818848, -7.307816505432129, 3.5977742671966553, -0.7911993861198425)
@@ -68,34 +71,86 @@
     return odd * ((order + 1) // 2) + (1 - odd) * (slabs - order // 2)
 
 
-def events_of(slabs):
+def scheduled_events(slabs, waves):
     timed = []
-    for order in range(1, slabs):
-        for chunk in range(CHUNKS):
-            q = (order - 1) * CHUNKS + chunk
-            timed += [(3 * q, (1, order, chunk)), (3 * q + 4, (2, order, chunk)), (3 * q + 6.5, (3, order, chunk))]
-        timed.append((3 * q + 6.75, (4, order, 0)))
-    return [event for _, event in sorted(timed)]
-
-
-def scheduled_events(slabs, waves):
-    plan, pending, reached = {}, [], 0
-    for event in events_of(slabs):
-        pending.append(event)
-        if event[0] == 4:
-            start = reached * waves
-            for i, early in enumerate(pending):
-                step = start + waves * (i + 1) // len(pending)
-                if reached == 0:
-                    step = 5 * waves // 8 if i == 0 else waves
-                plan.setdefault(step if early[0] != 4 else (reached + 1) * waves, []).append(early)
-            pending, reached = [], event[1]
+
+    def add(block, eighth, *event):
+        timed.append(((block * waves + eighth * waves // 8, eighth != 8, len(timed)), event))
+
+    for o in range(1, slabs):
+        if o == 1:
+            for eighth, event in ((2, (1, 1, 0)), (4, (1, 1, 1)), (5, (2, 1, 0)), (7, (2, 1, 1))):
+                add(0, eighth, *event)
+            add(0, 8, 3, 1, 0)
+            add(0, 8, 3, 1, 1)
+            add(0, 8, 4, 1, 0)
+        elif o == 2:
+            add(0, 7, 1, 2, 0)
+            add(0, 7, 1, 2, 1)
+            add(1, 0, 2, 2, 0)
+            add(1, 2, 2, 2, 1)
+            add(1, 2, 3, 2, 0)
+            add(1, 6, 3, 2, 1)
+            add(1, 8, 4, 2, 0)
+        else:
+            add(o - 2, 0, 1, o, 0)
+            add(o - 2, 5, 1, o, 1)
+            add(o - 2, 6, 2, o, 0)
+            add(o - 1, 0, 2, o, 1)
+            add(o - 1, 4, 3, o, 0)
+            add(o - 1, 4, 3, o, 1)
+            add(o - 1, 8, 4, o, 0)
+    plan = {}
+    for (step, *_), event in sorted(timed):
+        plan.setdefault(step, []).append(event)
     return plan
 
 
+def one_hot(targets, rows, columns):
+    row = lax.broadcasted_iota(jnp.int32, (rows, columns), 0)
+    wanted = jnp.zeros((rows, columns), jnp.int32)
+    for i, target in enumerate(targets):
+        wanted = jnp.where(row == i, target, wanted)
+    column = lax.broadcasted_iota(jnp.int32, (rows, columns), 1)
+    return (column == wanted).astype(jnp.float32).astype(jnp.bfloat16)
+
+
+def same_place(shape, row_shift, column_shift, row_mask=-1, column_mask=-1):
+    row = (lax.broadcasted_iota(jnp.int32, shape, 0) >> row_shift) & row_mask
+    column = (lax.broadcasted_iota(jnp.int32, shape, 1) >> column_shift) & column_mask
+    return (row == column).astype(jnp.float32)
+
+
+def last_with_last(a, b):
+    return lax.dot_general(a, b, (((1,), (1,)), ((), ())), preferred_element_type=jnp.float32)
+
+
+def gather_parameters(side, fields, templates, waves, count, coef_ref, sed_ref, index_ref, ids_ref, mix, weights):
+    bf16 = jnp.bfloat16
+    wanted = one_hot([index_ref[side * fields + f] for f in range(fields)], 8 * -(-fields // 8), coef_ref.shape[1])
+    coeffs = last_with_last(wanted, coef_ref[...])[:fields].astype(bf16)
+    bits = GROUP.bit_length() - 1
+    tall = same_place((fields * GROUP, fields), bits, 0).astype(bf16)
+    wide = same_place((count, count * GROUP), 0, bits).astype(bf16)
+    spread = jnp.dot(tall, coeffs, preferred_element_type=jnp.float32).astype(bf16)
+    spread = jnp.dot(spread, wide, preferred_element_type=jnp.float32)
+    mix[...] = (spread * same_place(spread.shape, 0, 0, GROUP - 1, GROUP - 1)).astype(bf16)
+
+    ids = [ids_ref[side * fields + f, j] for f in range(fields) for j in range(templates)]
+    wanted = one_hot(ids, fields * templates, sed_ref.shape[1])
+    table = sed_ref[...]
+    high = table.astype(bf16)
+    middle = (table - high.astype(jnp.float32)).astype(bf16)
+    low = (table - high.astype(jnp.float32) - middle.astype(jnp.float32)).astype(bf16)
+    raw = last_with_last(wanted, high) + last_with_last(wanted, middle) + last_with_last(wanted, low)
+    shares = (raw / jnp.sum(raw, axis=1, keepdims=True)).astype(bf16)
+    bits = PIX.bit_length() - 1
+    weights[...] = jnp.dot(shares, same_place((waves, waves * PIX), 0, bits).astype(bf16), preferred_element_type=jnp.float32)
+
+
 def psf_kernel(
-    sizes, waves, fields, share, mix_ref, weight_ref, length_ref, basis_ref, out_ref,
-    held, whole, inverse, path, image, tables, xtables, efield0, efield1, opening, power, total, arrived, staged,
+    sizes, waves, fields, share, coef_ref, sed_ref, index_ref, ids_ref, length_ref, basis_ref, out_ref,
+    mix, weights, held, whole, inverse, path, image, tables, xtables, efield0, efield1, opening, power, total, arrived, staged,
     local_sem, wl_send, wl_recv, send1, recv1, send2, recv2, send3, recv3, sum_send, sum_recv, out_send, out_recv,
 ):
     slabs, field_parts, group_parts = sizes
@@ -192,6 +247,8 @@
     for i in range(own_waves):
         inverse[me * own_waves + i] = 1.0 / jnp.full(inverse.shape[1:], length_ref[i], jnp.float32)
 
+    gather_parameters(side, fields, templates, waves, count, coef_ref, sed_ref, index_ref, ids_ref, mix, weights)
+
     def clear(f, carry):
         for l in range(waves):
             image[l, pl.ds(f * upix, upix), :] = jnp.zeros((upix, 2 * PUP), jnp.float32)
@@ -267,22 +324,25 @@
             field[...] = jnp.zeros_like(field)
 
     def slab_paths(slab):
-        mix = mix_ref[pl.ds(pl.multiple_of(side * fields * GROUP, GROUP), fields * GROUP), :]
-
         def paths(i, c):
-            pair = [whole[slab, pl.ds((2 * i + b) * count, count)].reshape(count * GROUP, LANES) for b in range(2)]
-            diff = jnp.dot(mix, jnp.concatenate(pair, axis=1), preferred_element_type=jnp.float32)
-            for b in range(2):
-                path[:, 2 * i + b] = diff[:, b * LANES : (b + 1) * LANES].reshape(fields, GROUP, LANES)
+            for q in range(BATCH // 2):
+                first = BATCH * i + 2 * q
+                pair = [whole[slab, pl.ds((first + b) * count, count)].reshape(count * GROUP, LANES) for b in range(2)]
+                diff = jnp.dot(mix[...], jnp.concatenate(pair, axis=1), preferred_element_type=jnp.float32)
+                for b in range(2):
+                    path[:, first + b] = diff[:, b * LANES : (b + 1) * LANES].reshape(fields, GROUP, LANES)
             return c
 
-        tile_pairs = 0
+        batches = 0
         for number, tiles in enumerate(layout):
-            tile_pairs = jnp.where(slab == number, (len(tiles) + 1) // 2, tile_pairs)
-        lax.fori_loop(0, tile_pairs, paths, 0)
-
-    def fill(field, tiles, f, inv):
+            batches = jnp.where(slab == number, -(-len(tiles) // BATCH), batches)
+        lax.fori_loop(0, batches, paths, 0)
+
+    def fill(field, tiles, f, inv, between=()):
         for t, (group, columns) in enumerate(tiles):
+            for i, work in enumerate(between):
+                if t == (2 * i + 1) * len(tiles) // (2 * len(between)):
+                    work()
             r = group * GROUP
             cosine, sine = turns_sincos(path[f, t] * inv, SHORT_SIN, SHORT_COS)
             cosine, sine = cosine.astype(jnp.bfloat16), sine.astype(jnp.bfloat16)
@@ -296,11 +356,16 @@
         inv = inverse[wave]
         return jnp.concatenate([inv[:, :LANES], inv[:, :LANES]], axis=0)
 
-    def accumulate(kernel, field, wave, f):
-        part_sum = jnp.dot(kernel, field[...], preferred_element_type=jnp.float32)
+    def accumulation(kernel, field, wave, f):
         here = pl.ds(f * upix, upix)
-        image[wave, here, :PUP] += part_sum[:upix]
-        image[wave, here, PUP:] += part_sum[upix:]
+
+        def part(n):
+            lanes = slice(n, n + WIDE)
+            part_sum = jnp.dot(kernel, field[:, lanes], preferred_element_type=jnp.float32)
+            image[wave, here, n : n + WIDE] += part_sum[:upix]
+            image[wave, here, PUP + n : PUP + n + WIDE] += part_sum[upix:]
+
+        return [functools.partial(part, n) for n in range(0, PUP, WIDE)]
 
     def handle(event):
         stage, o, c = event
@@ -357,11 +422,12 @@
         inv = inverse_tile(wave)
 
         def units(tiles):
+            work = []
             for f in range(fields):
-                fill(efields[f % 2], tiles, f, inv)
-                if f > 0:
-                    accumulate(kernel, efields[(f - 1) % 2], wave, f - 1)
-            accumulate(kernel, efields[(fields - 1) % 2], wave, fields - 1)
+                fill(efields[f % 2], tiles, f, inv, work)
+                work = accumulation(kernel, efields[f % 2], wave, f)
+            for rest in work:
+                rest()
 
         for number, tiles in enumerate(layout):
             pl.when(slab == number)(functools.partial(units, tiles))
@@ -395,39 +461,44 @@
         ref = out_ref.at[(1 - side) * fields + f]
         return remote(ref, ref, out_send.at[f], out_recv.at[f], partner)
 
-    def last_fields(f):
-        def two_waves(i, c):
+    def last_units(f):
+        def some_waves(i, c):
             def units(tiles):
-                for b in range(2):
-                    fill(efields[b], tiles, f, inverse_tile(2 * i + b))
-                    if b > 0:
-                        accumulate(xtables[2 * i], efield0, 2 * i, f)
-                accumulate(xtables[2 * i + 1], efield1, 2 * i + 1, f)
+                work = []
+                for b in range(AHEAD):
+                    wave = AHEAD * i + b
+                    fill(efields[b % 2], tiles, f, inverse_tile(wave), work)
+                    work = accumulation(xtables[wave], efields[b % 2], wave, f)
+                for rest in work:
+                    rest()
 
             for number, tiles in enumerate(layout):
                 pl.when(last == number)(functools.partial(units, tiles))
             return c
 
-        lax.fori_loop(0, waves // 2, two_waves, 0)
-
-        def finish(wave, c):
-            if not kept_tables:
-                second_table(wave, 0)
-            here = pl.ds(pl.multiple_of(f * upix, GROUP), upix)
-            field = jnp.dot(
-                image[wave, here, :].astype(jnp.bfloat16),
-                tables[wave if kept_tables else 0],
-                preferred_element_type=jnp.float32,
-            )
-            re, im = field[:, :PIX], field[:, PIX:]
-            bright = re * re + im * im
-            power[wave, here, :] = bright
-            total[f, pl.ds(wave, 1), :] = jnp.broadcast_to(
-                jnp.sum(jnp.sum(bright, axis=0, keepdims=True), axis=1, keepdims=True), (1, PIX)
-            )
+        lax.fori_loop(0, waves // AHEAD, some_waves, 0)
+
+    def last_images(f):
+        here = pl.ds(pl.multiple_of(f * upix, GROUP), upix)
+
+        def finish(i, c):
+            for b in range(AHEAD):
+                wave = AHEAD * i + b
+                if not kept_tables:
+                    second_table(wave, 0)
+                field = jnp.dot(
+                    image[wave, here, :].astype(jnp.bfloat16),
+                    tables[wave if kept_tables else 0],
+                    preferred_element_type=jnp.float32,
+                )
+                re, im = field[:, :PIX], field[:, PIX:]
+                bright = re * re + im * im
+                power[wave, here, :] = bright
+                total[f, pl.ds(wave, 1), :] = jnp.sum(bright, axis=0, keepdims=True)
             return c
 
-        lax.fori_loop(0, waves, finish, 0)
+        lax.fori_loop(0, waves // AHEAD, finish, 0)
+        total[f] = jnp.broadcast_to(jnp.sum(total[f], axis=1, keepdims=True), (waves, PIX))
         for d in range(1, pairs):
             sum_copy(f, d).start()
 
@@ -448,7 +519,7 @@
                     bright = power[l, pl.ds(pl.multiple_of(f * upix + first, step) + r, step), :]
                     spectrum = (bright * levels[l]).astype(jnp.bfloat16).astype(jnp.float32)
                     for j in range(templates):
-                        term = spectrum * weight_ref[((side * fields + f) * templates + j) * waves + l]
+                        term = spectrum * weights[pl.ds(f * templates + j, 1), l * PIX : (l + 1) * PIX]
                         sums[j] = term if l == 0 else sums[j] + term
                 for j in range(templates):
                     store(j, r, sums[j].astype(jnp.bfloat16))
@@ -467,12 +538,13 @@
         rows_of(side * (upix // 2), to_own)
 
     def tail(f, carry):
-        last_fields(f)
+        last_units(f)
 
         @pl.when(f > 0)
         def _():
             mix_field(f - 1)
 
+        last_images(f)
         return carry
 
     lax.fori_loop(0, fields, tail, 0)
@@ -500,14 +572,9 @@
     chips = field_parts * group_parts // 2
     tiles = max(len(t) for t in packed_tiles(slabs, rows))
     share = -(-tiles * count // (2 * CHUNKS * chips))
-    even = tiles + tiles % 2
+    even = -(-tiles // BATCH) * BATCH
     units = max(share * 2 * CHUNKS * chips, even * count)
 
-    coeffs = jnp.take(coef_table, table_index, axis=0, mode="clip")
-    same = jnp.eye(GROUP, dtype=jnp.bfloat16)
-    mix = (coeffs[:, None, :, None] * same[None, :, None, :]).reshape(fields * GROUP, -1)
-    raw = jnp.take(sed_table, template_ids, axis=0, mode="clip")
-    weights = (raw / jnp.sum(raw, axis=2, keepdims=True)).astype(jnp.bfloat16).astype(jnp.float32)
     hops = slabs - 1
     others = slabs // 2 - 1
     dma = pltpu.SemaphoreType.DMA
@@ -516,6 +583,8 @@
         functools.partial(psf_kernel, sizes, waves, half, share),
         in_specs=[
             pl.BlockSpec(memory_space=pltpu.VMEM),
+            pl.BlockSpec(memory_space=pltpu.VMEM),
+            pl.BlockSpec(memory_space=pltpu.SMEM),
             pl.BlockSpec(memory_space=pltpu.SMEM),
             pl.BlockSpec(memory_space=pltpu.SMEM),
             pl.BlockSpec(memory_space=pl.ANY),
@@ -523,6 +592,8 @@
         out_specs=pl.BlockSpec(memory_space=pltpu.VMEM),
         out_shape=jax.ShapeDtypeStruct((fields, templates, upix // 2, PIX), jnp.bfloat16),
         scratch_shapes=[
+            pltpu.VMEM((half * GROUP, count * GROUP), jnp.bfloat16),
+            pltpu.VMEM((half * templates, waves * PIX), jnp.float32),
             pltpu.VMEM((count, rows, PUP), jnp.bfloat16),
             pltpu.VMEM((slabs, units, GROUP, LANES), jnp.bfloat16),
             pltpu.VMEM((waves, 8, max(2 * rows, PIX)), jnp.float32),
@@ -554,7 +625,7 @@
         compiler_params=pltpu.CompilerParams(
             vmem_limit_bytes=60 * 2**20, collective_id=0, has_side_effects=True
         ),
-    )(mix, weights.reshape(-1), wave_lengths, mode_basis)
+    )(coef_table.T, sed_table.T, table_index, template_ids, wave_lengths, mode_basis)
 
 
 def solution(mesh):

time: 132 us -> 105 us (0.80)
  Pallas kernels: 121 us -> 102 us
  local copies, waits for them, and re-layouts: 9.54 us -> 3.16 us
    pallas_call x1, Pallas kernels: 121 us -> 102 us  [local(): pl.pallas_call(functools.partial(psf_kernel, sizes, waves, half, share),...]
    unnamed x3 -> x1, local copies, waits for them, and re-layouts: 5.54 us -> 3.16 us
where the time goes in v3:
time: 105 us
  Pallas kernels  102 us (97%)
  local copies, waits for them, and re-layouts  3.16 us (3%)
    pallas_call x1, Pallas kernels, local(): pl.pallas_call(functools.partial(psf_kernel, sizes, waves, half, share),...  102 us
    unnamed x1, local copies, waits for them, and re-layouts  3.16 us

profile of v3, /device:TPU:0, one launch (start us, length us, event | category | flops | bytes accessed | tf_op | source)
XLA Modules:
  0.0 105.0 jit_solution(6105895646452727818)
XLA Ops:
  0.0 101.8 %shard_map.64 = bf16[8,8,64,256]{3,2,1,0:T(8,128)(2,1)} custom-call(bf16[22,4096]{1,0:T(8,128)(2,1)} %bitcast.2, f32[8,1024]{1,0:T(8,128)} %bitcast.3, s32[8]{0:T(128)} %index_ref.1, s32[8,8]{1,0:T(8,128)} %ids_ref.1, f32[2]{0:T(128)} %length_ref.1, bf16[22,128,512]{2,1,0:T(8,128)(2,1)} %basis_ref.1), custom_call_target="tpu_custom_call" | custom-call | tf_op jit(solution)/shard_map/pallas_call | solution.py:582
  101.8 3.2 %copy.8 = bf16[8,8,64,256]{3,2,1,0:T(8,128)(2,1)} copy(bf16[8,8,64,256]{3,2,1,0:T(8,128)(2,1)} %shard_map.64) | data formatting | bytes 4194304

commit v4 on v3

--- a/solution.py
+++ b/solution.py
@@ -13,7 +13,6 @@
 EPSILON = 1e-06
 GROUP = 16
 LANES = 128
-WIDE = 256
 CHUNKS = 2
 AHEAD = 4
 BATCH = 6
@@ -79,14 +78,16 @@
 
     for o in range(1, slabs):
         if o == 1:
-            for eighth, event in ((2, (1, 1, 0)), (4, (1, 1, 1)), (5, (2, 1, 0)), (7, (2, 1, 1))):
+            for eighth, event in ((0, (1, 1, 0)), (1, (1, 1, 1)), (4, (2, 1, 0)), (6, (2, 1, 1)), (7, (3, 1, 0))):
                 add(0, eighth, *event)
-            add(0, 8, 3, 1, 0)
+            if slabs > 2:
+                add(0, 7, 1, 2, 0)
             add(0, 8, 3, 1, 1)
+            if slabs > 2:
+                add(0, 8, 1, 2, 1)
+            add(0, 8, 0, 1, 0)
             add(0, 8, 4, 1, 0)
         elif o == 2:
-            add(0, 7, 1, 2, 0)
-            add(0, 7, 1, 2, 1)
             add(1, 0, 2, 2, 0)
             add(1, 2, 2, 2, 1)
             add(1, 2, 3, 2, 0)
@@ -150,7 +151,7 @@
 
 def psf_kernel(
     sizes, waves, fields, share, coef_ref, sed_ref, index_ref, ids_ref, length_ref, basis_ref, out_ref,
-    mix, weights, held, whole, inverse, path, image, tables, xtables, efield0, efield1, opening, power, total, arrived, staged,
+    mix, weights, held, whole, inverse, path, image, tables, xtables, efields, opening, power, total, arrived, staged,
     local_sem, wl_send, wl_recv, send1, recv1, send2, recv2, send3, recv3, sum_send, sum_recv, out_send, out_recv,
 ):
     slabs, field_parts, group_parts = sizes
@@ -247,14 +248,11 @@
     for i in range(own_waves):
         inverse[me * own_waves + i] = 1.0 / jnp.full(inverse.shape[1:], length_ref[i], jnp.float32)
 
-    gather_parameters(side, fields, templates, waves, count, coef_ref, sed_ref, index_ref, ids_ref, mix, weights)
-
     def clear(f, carry):
         for l in range(waves):
             image[l, pl.ds(f * upix, upix), :] = jnp.zeros((upix, 2 * PUP), jnp.float32)
         return carry
 
-    lax.fori_loop(0, fields, clear, 0)
     bring.wait()
 
     low_lanes = (lax.broadcasted_iota(jnp.int32, (GROUP, LANES), 1) < LANES // 2).astype(jnp.float32)
@@ -281,6 +279,8 @@
         first_copy(1, c).start()
     for d in range(1, slabs):
         length_copy(d, me).start()
+    gather_parameters(side, fields, templates, waves, count, coef_ref, sed_ref, index_ref, ids_ref, mix, weights)
+    lax.fori_loop(0, fields, clear, 0)
     for d in range(1, slabs):
         length_copy(d, (me + slabs - d) % slabs).wait_recv()
 
@@ -298,15 +298,13 @@
             tables[slot, PUP + r : PUP + r + step, PIX:] = cosine
 
     def x_table(slab, wave):
-        lane = lax.broadcasted_iota(jnp.int32, (upix, 2 * rows), 1)
-        real = lane < rows
-        xs = 2 * (slab * rows + jnp.where(real, lane, lane - rows)) - PUP + 1
-        us = first_pix + lax.broadcasted_iota(jnp.int32, (upix, 2 * rows), 0) - PIX // 2
-        scale = inverse[wave][:1, : 2 * rows] * (0.25 / (2.0 * PUP))
+        xs = 2 * (slab * rows + lax.broadcasted_iota(jnp.int32, (upix, rows), 1)) - PUP + 1
+        us = first_pix + lax.broadcasted_iota(jnp.int32, (upix, rows), 0) - PIX // 2
+        scale = inverse[wave][:1, :rows] * (0.25 / (2.0 * PUP))
         cosine, sine = turns_sincos((us * xs).astype(jnp.float32) * scale)
-        return jnp.concatenate(
-            [jnp.where(real, cosine, sine), jnp.where(real, -sine, cosine)], axis=0
-        ).astype(jnp.bfloat16)
+        upper = jnp.concatenate([cosine, sine], axis=1)
+        lower = jnp.concatenate([-sine, cosine], axis=1)
+        return jnp.concatenate([upper, lower], axis=0).astype(jnp.bfloat16)
 
     def open_slab(slab):
         def openings(g, c):
@@ -320,8 +318,8 @@
             return c
 
         lax.fori_loop(0, rows // GROUP, openings, 0)
-        for field in (efield0, efield1):
-            field[...] = jnp.zeros_like(field)
+        for i in range(efields.shape[0]):
+            efields[i] = jnp.zeros(efields.shape[1:], efields.dtype)
 
     def slab_paths(slab):
         def paths(i, c):
@@ -338,37 +336,35 @@
             batches = jnp.where(slab == number, -(-len(tiles) // BATCH), batches)
         lax.fori_loop(0, batches, paths, 0)
 
-    def fill(field, tiles, f, inv, between=()):
+    def fill(field, tiles, f, inv):
         for t, (group, columns) in enumerate(tiles):
-            for i, work in enumerate(between):
-                if t == (2 * i + 1) * len(tiles) // (2 * len(between)):
-                    work()
             r = group * GROUP
             cosine, sine = turns_sincos(path[f, t] * inv, SHORT_SIN, SHORT_COS)
             cosine, sine = cosine.astype(jnp.bfloat16), sine.astype(jnp.bfloat16)
             for c in columns:
                 lanes = slice(c * LANES, (c + 1) * LANES)
                 hole = opening[r : r + GROUP, lanes]
-                field[r : r + GROUP, lanes] = cosine * hole
-                field[rows + r : rows + r + GROUP, lanes] = sine * hole
+                efields[field, r : r + GROUP, lanes] = cosine * hole
+                efields[field, rows + r : rows + r + GROUP, lanes] = sine * hole
 
     def inverse_tile(wave):
         inv = inverse[wave]
         return jnp.concatenate([inv[:, :LANES], inv[:, :LANES]], axis=0)
 
-    def accumulation(kernel, field, wave, f):
+    def accumulate(kernel, field, wave, f):
+        part_sum = jnp.dot(kernel, efields[field], preferred_element_type=jnp.float32)
         here = pl.ds(f * upix, upix)
-
-        def part(n):
-            lanes = slice(n, n + WIDE)
-            part_sum = jnp.dot(kernel, field[:, lanes], preferred_element_type=jnp.float32)
-            image[wave, here, n : n + WIDE] += part_sum[:upix]
-            image[wave, here, PUP + n : PUP + n + WIDE] += part_sum[upix:]
-
-        return [functools.partial(part, n) for n in range(0, PUP, WIDE)]
+        image[wave, here, :PUP] += part_sum[:upix]
+        image[wave, here, PUP:] += part_sum[upix:]
 
     def handle(event):
         stage, o, c = event
+        if stage == 0 and kept_tables:
+            def make(l, carry):
+                second_table(l, l)
+                return carry
+
+            lax.fori_loop(0, waves, make, 0)
         if stage == 1:
             first_landed(o, c).wait_recv()
             for e in range(1, 3 if relay else chips):
@@ -386,7 +382,6 @@
             for each in range(CHUNKS):
                 core_copy(o, each, 1 - core).wait_recv()
 
-    efields = (efield0, efield1)
     plan = scheduled_events(slabs, waves)
     last_step = (slabs - 1) * waves
 
@@ -395,16 +390,6 @@
         wave = step % waves
         slab = from_slab(order)
 
-        if kept_tables:
-
-            @pl.when(step == waves)
-            def _():
-                def make(l, c):
-                    second_table(l, l)
-                    return c
-
-                lax.fori_loop(0, waves, make, 0)
-
         for at, events in plan.items():
             if at < last_step:
 
@@ -422,12 +407,10 @@
         inv = inverse_tile(wave)
 
         def units(tiles):
-            work = []
             for f in range(fields):
-                fill(efields[f % 2], tiles, f, inv, work)
-                work = accumulation(kernel, efields[f % 2], wave, f)
-            for rest in work:
-                rest()
+                fill(f, tiles, f, inv)
+            for f in range(fields):
+                accumulate(kernel, f, wave, f)
 
         for number, tiles in enumerate(layout):
             pl.when(slab == number)(functools.partial(units, tiles))
@@ -464,13 +447,10 @@
     def last_units(f):
         def some_waves(i, c):
             def units(tiles):
-                work = []
                 for b in range(AHEAD):
-                    wave = AHEAD * i + b
-                    fill(efields[b % 2], tiles, f, inverse_tile(wave), work)
-                    work = accumulation(xtables[wave], efields[b % 2], wave, f)
-                for rest in work:
-                    rest()
+                    fill(b, tiles, f, inverse_tile(AHEAD * i + b))
+                for b in range(AHEAD):
+                    accumulate(xtables[AHEAD * i + b], b, AHEAD * i + b, f)
 
             for number, tiles in enumerate(layout):
                 pl.when(last == number)(functools.partial(units, tiles))
@@ -601,8 +581,7 @@
             pltpu.VMEM((waves, half * upix, 2 * PUP), jnp.float32),
             pltpu.VMEM((waves if waves <= 8 else 1, 2 * PUP, 2 * PIX), jnp.bfloat16),
             pltpu.VMEM((waves, 2 * upix, 2 * rows), jnp.bfloat16),
-            pltpu.VMEM((2 * rows, PUP), jnp.bfloat16),
-            pltpu.VMEM((2 * rows, PUP), jnp.bfloat16),
+            pltpu.VMEM((max(half, AHEAD), 2 * rows, PUP), jnp.bfloat16),
             pltpu.VMEM((rows, PUP), jnp.bfloat16),
             pltpu.VMEM((waves, half * upix, PIX), jnp.float32),
             pltpu.VMEM((half, waves, PIX), jnp.float32),

time: 105 us -> 102 us (0.971)
  Pallas kernels: 102 us -> 98.3 us
    pallas_call x1, Pallas kernels: 102 us -> 98.3 us  [local(): pl.pallas_call(functools.partial(psf_kernel, sizes, waves, half, share),...]
where the time goes in v4:
time: 102 us
  Pallas kernels  98.3 us (96%)
  local copies, waits for them, and re-layouts  3.16 us (3%)
    pallas_call x1, Pallas kernels, local(): pl.pallas_call(functools.partial(psf_kernel, sizes, waves, half, share),...  98.3 us
    unnamed x1, local copies, waits for them, and re-layouts  3.16 us

profile of v4, /device:TPU:0, one launch (start us, length us, event | category | flops | bytes accessed | tf_op | source)
XLA Modules:
  0.0 101.5 jit_solution(5336699765145225899)
XLA Ops:
  0.0 98.3 %shard_map.64 = bf16[8,8,64,256]{3,2,1,0:T(8,128)(2,1)} custom-call(bf16[22,4096]{1,0:T(8,128)(2,1)} %bitcast.2, f32[8,1024]{1,0:T(8,128)} %bitcast.3, s32[8]{0:T(128)} %index_ref.1, s32[8,8]{1,0:T(8,128)} %ids_ref.1, f32[2]{0:T(128)} %length_ref.1, bf16[22,128,512]{2,1,0:T(8,128)(2,1)} %basis_ref.1), custom_call_target="tpu_custom_call" | custom-call | tf_op jit(solution)/shard_map/pallas_call | solution.py:562
  98.3 3.2 %copy.8 = bf16[8,8,64,256]{3,2,1,0:T(8,128)(2,1)} copy(bf16[8,8,64,256]{3,2,1,0:T(8,128)(2,1)} %shard_map.64) | data formatting | bytes 4194304

commit v5 on v4

--- a/solution.py
+++ b/solution.py
@@ -137,8 +137,8 @@
     spread = jnp.dot(spread, wide, preferred_element_type=jnp.float32)
     mix[...] = (spread * same_place(spread.shape, 0, 0, GROUP - 1, GROUP - 1)).astype(bf16)
 
-    ids = [ids_ref[side * fields + f, j] for f in range(fields) for j in range(templates)]
-    wanted = one_hot(ids, fields * templates, sed_ref.shape[1])
+    ids = [ids_ref[f, j] for f in range(2 * fields) for j in range(templates)]
+    wanted = one_hot(ids, 2 * fields * templates, sed_ref.shape[1])
     table = sed_ref[...]
     high = table.astype(bf16)
     middle = (table - high.astype(jnp.float32)).astype(bf16)
@@ -151,14 +151,13 @@
 
 def psf_kernel(
     sizes, waves, fields, share, coef_ref, sed_ref, index_ref, ids_ref, length_ref, basis_ref, out_ref,
-    mix, weights, held, whole, inverse, path, image, tables, xtables, efields, opening, power, total, arrived, staged,
+    mix, weights, held, whole, inverse, path, image, tables, xtables, efields, opening, power, total, arrived, incoming,
     local_sem, wl_send, wl_recv, send1, recv1, send2, recv2, send3, recv3, sum_send, sum_recv, out_send, out_recv,
 ):
     slabs, field_parts, group_parts = sizes
     count, rows, _ = basis_ref.shape
     upix = 2 * PIX // slabs
     own_waves = waves // slabs
-    pairs = slabs // 2
     x_parts = field_parts // 2
     chips = x_parts * group_parts
     templates = out_ref.shape[1]
@@ -433,16 +432,10 @@
 
     def sum_copy(f, shift):
         at = (f, shift - 1)
-        return remote(
-            total.at[f], arrived.at[shift - 1, f], sum_send.at[at], sum_recv.at[at], {"wave": (me + 2 * shift) % slabs}
-        )
-
-    def out_copy(f):
-        return remote(staged.at[f], out_ref.at[side * fields + f], out_send.at[f], out_recv.at[f], partner)
-
-    def out_landed(f):
-        ref = out_ref.at[(1 - side) * fields + f]
-        return remote(ref, ref, out_send.at[f], out_recv.at[f], partner)
+        return remote(total.at[f], arrived.at[shift - 1, f], sum_send.at[at], sum_recv.at[at], wave_peer(shift))
+
+    def exchange(f):
+        return remote(power.at[f, 1 - side], incoming.at[f], out_send.at[f], out_recv.at[f], partner)
 
     def last_units(f):
         def some_waves(i, c):
@@ -473,65 +466,69 @@
                 )
                 re, im = field[:, :PIX], field[:, PIX:]
                 bright = re * re + im * im
-                power[wave, here, :] = bright
+                for h in range(2):
+                    power[f, h, wave] = bright[h * upix // 2 : (h + 1) * upix // 2].astype(jnp.bfloat16)
                 total[f, pl.ds(wave, 1), :] = jnp.sum(bright, axis=0, keepdims=True)
             return c
 
         lax.fori_loop(0, waves // AHEAD, finish, 0)
         total[f] = jnp.broadcast_to(jnp.sum(total[f], axis=1, keepdims=True), (waves, PIX))
-        for d in range(1, pairs):
+        for d in range(1, slabs):
             sum_copy(f, d).start()
-
-    def mix_field(f):
-        everything = total[f]
-        for d in range(1, pairs):
-            sum_copy(f, d).wait()
-            everything = everything + arrived[d - 1, f]
+        exchange(f).start()
+
+    def mix_field(field, everything, source):
         level_all = 1.0 / (everything * (1.0 / (PIX * PIX)) + EPSILON)
         levels = [level_all[l : l + 1, :] for l in range(waves)]
         step = 16
 
-        def rows_of(first, store):
-            def chunk(i, c):
-                r = pl.multiple_of(i * step, step)
-                sums = [None] * templates
-                for l in range(waves):
-                    bright = power[l, pl.ds(pl.multiple_of(f * upix + first, step) + r, step), :]
-                    spectrum = (bright * levels[l]).astype(jnp.bfloat16).astype(jnp.float32)
-                    for j in range(templates):
-                        term = spectrum * weights[pl.ds(f * templates + j, 1), l * PIX : (l + 1) * PIX]
-                        sums[j] = term if l == 0 else sums[j] + term
+        def chunk(i, c):
+            r = pl.multiple_of(i * step, step)
+            sums = [None] * templates
+            for l in range(waves):
+                spectrum = source[l, pl.ds(r, step), :].astype(jnp.float32) * levels[l]
                 for j in range(templates):
-                    store(j, r, sums[j].astype(jnp.bfloat16))
-                return c
-
-            lax.fori_loop(0, upix // 2 // step, chunk, 0)
-
-        def to_partner(j, r, value):
-            staged[f, j, pl.ds(r, step), :] = value
-
-        def to_own(j, r, value):
-            out_ref[side * fields + f, j, pl.ds(r, step), :] = value
-
-        rows_of((1 - side) * (upix // 2), to_partner)
-        out_copy(f).start()
-        rows_of(side * (upix // 2), to_own)
+                    term = spectrum * weights[pl.ds(field * templates + j, 1), l * PIX : (l + 1) * PIX]
+                    sums[j] = term if l == 0 else sums[j] + term
+            for j in range(templates):
+                out_ref[field, j, pl.ds(r, step), :] = sums[j].astype(jnp.bfloat16)
+            return c
+
+        lax.fori_loop(0, upix // 2 // step, chunk, 0)
+
+    def mix_own(f):
+        everything = total[f]
+        for d in range(2, slabs, 2):
+            sum_copy(f, d).wait()
+            everything = everything + arrived[d - 1, f]
+        mix_field(side * fields + f, everything, power.at[f, side])
+
+    def mix_other(f):
+        everything = None
+        for d in range(1, slabs, 2):
+            sum_copy(f, d).wait()
+            everything = arrived[d - 1, f] if d == 1 else everything + arrived[d - 1, f]
+        exchange(f).wait()
+        mix_field((1 - side) * fields + f, everything, incoming.at[f])
 
     def tail(f, carry):
         last_units(f)
 
         @pl.when(f > 0)
         def _():
-            mix_field(f - 1)
+            mix_own(f - 1)
+
+        @pl.when(f > 1)
+        def _():
+            mix_other(f - 2)
 
         last_images(f)
         return carry
 
     lax.fori_loop(0, fields, tail, 0)
-    mix_field(fields - 1)
-    for f in range(fields):
-        out_landed(f).wait_recv()
-        out_copy(f).wait_send()
+    mix_own(fields - 1)
+    for f in range(max(fields - 2, 0), fields):
+        mix_other(f)
 
     for d in range(1, slabs):
         length_copy(d, me).wait_send()
@@ -556,7 +553,6 @@
     units = max(share * 2 * CHUNKS * chips, even * count)
 
     hops = slabs - 1
-    others = slabs // 2 - 1
     dma = pltpu.SemaphoreType.DMA
 
     return pl.pallas_call(
@@ -573,7 +569,7 @@
         out_shape=jax.ShapeDtypeStruct((fields, templates, upix // 2, PIX), jnp.bfloat16),
         scratch_shapes=[
             pltpu.VMEM((half * GROUP, count * GROUP), jnp.bfloat16),
-            pltpu.VMEM((half * templates, waves * PIX), jnp.float32),
+            pltpu.VMEM((fields * templates, waves * PIX), jnp.float32),
             pltpu.VMEM((count, rows, PUP), jnp.bfloat16),
             pltpu.VMEM((slabs, units, GROUP, LANES), jnp.bfloat16),
             pltpu.VMEM((waves, 8, max(2 * rows, PIX)), jnp.float32),
@@ -583,10 +579,10 @@
             pltpu.VMEM((waves, 2 * upix, 2 * rows), jnp.bfloat16),
             pltpu.VMEM((max(half, AHEAD), 2 * rows, PUP), jnp.bfloat16),
             pltpu.VMEM((rows, PUP), jnp.bfloat16),
-            pltpu.VMEM((waves, half * upix, PIX), jnp.float32),
+            pltpu.VMEM((half, 2, waves, upix // 2, PIX), jnp.bfloat16),
             pltpu.VMEM((half, waves, PIX), jnp.float32),
-            pltpu.VMEM((others, half, waves, PIX), jnp.float32),
-            pltpu.VMEM((half, templates, upix // 2, PIX), jnp.bfloat16),
+            pltpu.VMEM((hops, half, waves, PIX), jnp.float32),
+            pltpu.VMEM((half, waves, upix // 2, PIX), jnp.bfloat16),
             dma,
             dma((hops,)),
             dma((hops,)),
@@ -596,8 +592,8 @@
             dma((hops, CHUNKS, chips - 1)),
             dma((hops, CHUNKS)),
             dma((hops, CHUNKS)),
-            dma((half, others)),
-            dma((half, others)),
+            dma((half, hops)),
+            dma((half, hops)),
             dma((half,)),
             dma((half,)),
         ],

time: 102 us -> 96.6 us (0.947)
  Pallas kernels: 98.3 us -> 93.2 us
    pallas_call x1, Pallas kernels: 98.3 us -> 93.2 us  [local(): pl.pallas_call(functools.partial(psf_kernel, sizes, waves, half, share),...]
where the time goes in v5:
time: 96.6 us; the launch traced here: 96.4 us
  Pallas kernels  93.2 us (96%)
  local copies, waits for them, and re-layouts  3.16 us (3%)
    pallas_call x1, Pallas kernels, local(): pl.pallas_call(functools.partial(psf_kernel, sizes, waves, half, share),...  93.2 us
    unnamed x1, local copies, waits for them, and re-layouts  3.16 us

profile of v5, /device:TPU:0, one launch (start us, length us, event | category | flops | bytes accessed | tf_op | source)
XLA Modules:
  0.0 96.4 jit_solution(3827832812091227592)
XLA Ops:
  0.0 93.2 %shard_map.64 = bf16[8,8,64,256]{3,2,1,0:T(8,128)(2,1)} custom-call(bf16[22,4096]{1,0:T(8,128)(2,1)} %bitcast.2, f32[8,1024]{1,0:T(8,128)} %bitcast.3, s32[8]{0:T(128)} %index_ref.1, s32[8,8]{1,0:T(8,128)} %ids_ref.1, f32[2]{0:T(128)} %length_ref.1, bf16[22,128,512]{2,1,0:T(8,128)(2,1)} %basis_ref.1), custom_call_target="tpu_custom_call" | custom-call | tf_op jit(solution)/shard_map/pallas_call | solution.py:558
  93.2 3.2 %copy.8 = bf16[8,8,64,256]{3,2,1,0:T(8,128)(2,1)} copy(bf16[8,8,64,256]{3,2,1,0:T(8,128)(2,1)} %shard_map.64) | data formatting | bytes 4194304

commit v6 on v5

--- a/solution.py
+++ b/solution.py
@@ -16,12 +16,13 @@
 CHUNKS = 2
 AHEAD = 4
 BATCH = 6
+LIMIT = 54
 ROUNDER = 12582912.0
 
 SIN = (4.442879676818848, -7.307816505432129, 3.5977742671966553, -0.7911993861198425)
 COS = (1.4142135381698608, -6.978850841522217, 5.739460468292236, -1.883557915687561, 0.3106880187988281)
 SHORT_SIN = (4.440917015075684, -7.256804466247559, 3.229630470275879)
-SHORT_COS = (1.414183259010315, -6.976953506469727, 5.709674835205078, -1.7155721187591553)
+SHORT_COS = (1.4140625, -6.96875, 5.65625, -1.7265625)
 
 
 def horner(coefficients, s):
@@ -38,6 +39,15 @@
     a = r * horner(sine, s)
     b = horner(cosine, s)
     return 1.0 - a * a, a * b
+
+
+def rounded_sincos(turns):
+    nearest = (turns + ROUNDER) - ROUNDER
+    r = turns - nearest
+    s = r * r
+    a = r * horner(SHORT_SIN, s)
+    b = horner([jnp.bfloat16(c) for c in SHORT_COS], s.astype(jnp.bfloat16))
+    return (1.0 - a * a).astype(jnp.bfloat16), a.astype(jnp.bfloat16) * b
 
 
 def packed_tiles(slabs, rows):
@@ -151,8 +161,8 @@
 
 def psf_kernel(
     sizes, waves, fields, share, coef_ref, sed_ref, index_ref, ids_ref, length_ref, basis_ref, out_ref,
-    mix, weights, held, whole, inverse, path, image, tables, xtables, efields, opening, power, total, arrived, incoming,
-    local_sem, wl_send, wl_recv, send1, recv1, send2, recv2, send3, recv3, sum_send, sum_recv, out_send, out_recv,
+    mix, weights, held, whole, inverse, path, image, tables, xtables, efields, opening, power, total, arrived, incoming, mixed,
+    local_sem, wl_send, wl_recv, send1, recv1, send2, recv2, send3, recv3, sum_send, sum_recv, out_send, out_recv, result_sem,
 ):
     slabs, field_parts, group_parts = sizes
     count, rows, _ = basis_ref.shape
@@ -338,8 +348,7 @@
     def fill(field, tiles, f, inv):
         for t, (group, columns) in enumerate(tiles):
             r = group * GROUP
-            cosine, sine = turns_sincos(path[f, t] * inv, SHORT_SIN, SHORT_COS)
-            cosine, sine = cosine.astype(jnp.bfloat16), sine.astype(jnp.bfloat16)
+            cosine, sine = rounded_sincos(path[f, t] * inv)
             for c in columns:
                 lanes = slice(c * LANES, (c + 1) * LANES)
                 hole = opening[r : r + GROUP, lanes]
@@ -491,10 +500,14 @@
                     term = spectrum * weights[pl.ds(field * templates + j, 1), l * PIX : (l + 1) * PIX]
                     sums[j] = term if l == 0 else sums[j] + term
             for j in range(templates):
-                out_ref[field, j, pl.ds(r, step), :] = sums[j].astype(jnp.bfloat16)
+                mixed[field, j, pl.ds(r, step), :] = sums[j].astype(jnp.bfloat16)
             return c
 
         lax.fori_loop(0, upix // 2 // step, chunk, 0)
+        result_copy(field).start()
+
+    def result_copy(field):
+        return pltpu.make_async_copy(mixed.at[field], out_ref.at[field], result_sem.at[field])
 
     def mix_own(f):
         everything = total[f]
@@ -530,6 +543,8 @@
     for f in range(max(fields - 2, 0), fields):
         mix_other(f)
 
+    for field in range(2 * fields):
+        result_copy(field).wait()
     for d in range(1, slabs):
         length_copy(d, me).wait_send()
     for o in range(1, slabs):
@@ -565,7 +580,7 @@
             pl.BlockSpec(memory_space=pltpu.SMEM),
             pl.BlockSpec(memory_space=pl.ANY),
         ],
-        out_specs=pl.BlockSpec(memory_space=pltpu.VMEM),
+        out_specs=pl.BlockSpec(memory_space=pl.ANY),
         out_shape=jax.ShapeDtypeStruct((fields, templates, upix // 2, PIX), jnp.bfloat16),
         scratch_shapes=[
             pltpu.VMEM((half * GROUP, count * GROUP), jnp.bfloat16),
@@ -583,6 +598,7 @@
             pltpu.VMEM((half, waves, PIX), jnp.float32),
             pltpu.VMEM((hops, half, waves, PIX), jnp.float32),
             pltpu.VMEM((half, waves, upix // 2, PIX), jnp.bfloat16),
+            pltpu.VMEM((fields, templates, upix // 2, PIX), jnp.bfloat16),
             dma,
             dma((hops,)),
             dma((hops,)),
@@ -596,9 +612,10 @@
             dma((half, hops)),
             dma((half,)),
             dma((half,)),
+            dma((fields,)),
         ],
         compiler_params=pltpu.CompilerParams(
-            vmem_limit_bytes=60 * 2**20, collective_id=0, has_side_effects=True
+            vmem_limit_bytes=LIMIT * 2**20, collective_id=0, has_side_effects=True
         ),
     )(coef_table.T, sed_table.T, table_index, template_ids, wave_lengths, mode_basis)
 

time: 96.6 us -> 94.5 us (0.978)
  Pallas kernels: 93.2 us -> 91.1 us
    pallas_call x1, Pallas kernels: 93.2 us -> 91.1 us  [local(): pl.pallas_call(functools.partial(psf_kernel, sizes, waves, half, share),...]
where the time goes in v6:
time: 94.5 us; the launch traced here: 94.3 us
  Pallas kernels  91.1 us (96%)
  local copies, waits for them, and re-layouts  3.16 us (3%)
    pallas_call x1, Pallas kernels, local(): pl.pallas_call(functools.partial(psf_kernel, sizes, waves, half, share),...  91.1 us
    unnamed x1, local copies, waits for them, and re-layouts  3.16 us

profile of v6, /device:TPU:0, one launch (start us, length us, event | category | flops | bytes accessed | tf_op | source)
XLA Modules:
  0.0 94.3 jit_solution(11512341029660411112)
XLA Ops:
  0.0 91.1 %shard_map.64 = bf16[8,8,64,256]{3,2,1,0:T(8,128)(2,1)} custom-call(bf16[22,4096]{1,0:T(8,128)(2,1)} %bitcast.2, f32[8,1024]{1,0:T(8,128)} %bitcast.3, s32[8]{0:T(128)} %index_ref.1, s32[8,8]{1,0:T(8,128)} %ids_ref.1, f32[2]{0:T(128)} %length_ref.1, bf16[22,128,512]{2,1,0:T(8,128)(2,1)} %basis_ref.1), custom_call_target="tpu_custom_call" | custom-call | tf_op jit(solution)/shard_map/pallas_call | solution.py:573
  91.2 3.2 %copy.8 = bf16[8,8,64,256]{3,2,1,0:T(8,128)(2,1)} copy(bf16[8,8,64,256]{3,2,1,0:T(8,128)(2,1)} %shard_map.64) | data formatting | bytes 4194304

commit v7 on v6

--- a/solution.py
+++ b/solution.py
@@ -14,7 +14,7 @@
 GROUP = 16
 LANES = 128
 CHUNKS = 2
-AHEAD = 4
+AHEAD = 8
 BATCH = 6
 LIMIT = 54
 ROUNDER = 12582912.0
@@ -62,15 +62,16 @@
         for group in range(rows // GROUP):
             first = slab * rows + group * GROUP
             need = inside[first : first + GROUP].any(axis=0).reshape(columns, LANES)
+            full = inside[first : first + GROUP].all(axis=0).reshape(columns, LANES).all(axis=1)
             low, high = need[:, :half].any(axis=1), need[:, half:].any(axis=1)
             lows = [c for c in range(columns) if low[c] and not high[c]]
             highs = [c for c in range(columns) if high[c] and not low[c]]
             pairs = list(zip(lows, highs))
             for c in range(columns):
                 if low[c] and high[c]:
-                    tiles.append((group, (c,)))
-            tiles += [(group, pair) for pair in pairs]
-            tiles += [(group, (c,)) for c in lows[len(pairs) :] + highs[len(pairs) :]]
+                    tiles.append((group, (c,), bool(full[c])))
+            tiles += [(group, pair, False) for pair in pairs]
+            tiles += [(group, (c,), False) for c in lows[len(pairs) :] + highs[len(pairs) :]]
         result.append(tuple(tiles))
     return result
 
@@ -268,7 +269,7 @@
     low_lanes, high_lanes = low_lanes.astype(jnp.bfloat16), (1.0 - low_lanes).astype(jnp.bfloat16)
 
     def pack(tiles, k, carry):
-        for t, (group, columns) in enumerate(tiles):
+        for t, (group, columns, full) in enumerate(tiles):
             r = group * GROUP
             parts = [held[k, r : r + GROUP, c * LANES : (c + 1) * LANES] for c in columns]
             value = parts[0]
@@ -346,14 +347,14 @@
         lax.fori_loop(0, batches, paths, 0)
 
     def fill(field, tiles, f, inv):
-        for t, (group, columns) in enumerate(tiles):
+        for t, (group, columns, full) in enumerate(tiles):
             r = group * GROUP
             cosine, sine = rounded_sincos(path[f, t] * inv)
             for c in columns:
                 lanes = slice(c * LANES, (c + 1) * LANES)
-                hole = opening[r : r + GROUP, lanes]
-                efields[field, r : r + GROUP, lanes] = cosine * hole
-                efields[field, rows + r : rows + r + GROUP, lanes] = sine * hole
+                hole = None if full else opening[r : r + GROUP, lanes]
+                efields[field, r : r + GROUP, lanes] = cosine if full else cosine * hole
+                efields[field, rows + r : rows + r + GROUP, lanes] = sine if full else sine * hole
 
     def inverse_tile(wave):
         inv = inverse[wave]

time: 94.5 us -> 94.4 us (level)
  no operation moved by 1% of the time
where the time goes in v7:
time: 94.4 us; the launch traced here: 94.2 us
  Pallas kernels  91.1 us (97%)
  local copies, waits for them, and re-layouts  3.16 us (3%)
    pallas_call x1, Pallas kernels, local(): pl.pallas_call(functools.partial(psf_kernel, sizes, waves, half, share),...  91.1 us
    unnamed x1, local copies, waits for them, and re-layouts  3.16 us

profile of v7, /device:TPU:0, one launch (start us, length us, event | category | flops | bytes accessed | tf_op | source)
XLA Modules:
  0.0 94.2 jit_solution(9083800708153184359)
XLA Ops:
  0.0 91.1 %shard_map.64 = bf16[8,8,64,256]{3,2,1,0:T(8,128)(2,1)} custom-call(bf16[22,4096]{1,0:T(8,128)(2,1)} %bitcast.2, f32[8,1024]{1,0:T(8,128)} %bitcast.3, s32[8]{0:T(128)} %index_ref.1, s32[8,8]{1,0:T(8,128)} %ids_ref.1, f32[2]{0:T(128)} %length_ref.1, bf16[22,128,512]{2,1,0:T(8,128)(2,1)} %basis_ref.1), custom_call_target="tpu_custom_call" | custom-call | tf_op jit(solution)/shard_map/pallas_call | solution.py:574
  91.1 3.2 %copy.8 = bf16[8,8,64,256]{3,2,1,0:T(8,128)(2,1)} copy(bf16[8,8,64,256]{3,2,1,0:T(8,128)(2,1)} %shard_map.64) | data formatting | bytes 4194304
